TPU v7x, 128 devices: a whole 4x4x4 slice. The times are simulated.
128 devices in a mesh: owner: 64 (over z, y, x), sub: 2 (over core).
Axes of the slice: x: 4, y: 4, z: 4, core: 2. Of those that a mesh axis runs over, the one named last changes fastest.
Arguments:
- file_fields: bfloat16 [131072, 2560], P(('owner', 'sub')), may hold values from -6 to 6
- span_map: int32 [128, 128], P(('owner', 'sub')), may hold values from 0 to 127, each once within a row
- point_dest: int32 [2097152, 1], P(('owner', 'sub')), may hold values from 0 to 127; in each aligned block of 16384 rows (0 to 16383, 16384 to 32767, ...) at most 256 rows name the same one
- point_local: int32 [2097152], P(('owner', 'sub')), may hold values from 0 to 1023, as said below
- point_coords: float32 [3, 2097152], P(None, ('owner', 'sub')), may hold values from -1 to 1
Outputs:
- point_values: float32 [5, 2097152], P(None, ('owner', 'sub'))
- owned: bfloat16 [131072, 2560], P(('owner', 'sub'))
Inputs may be any that keep to these rules, and one draw needn't show every extreme that they name: `point_dest`: among the 16384 points of one device at most 256 name one owner, a bound that some blocks reach. `span_map`: each row is a permutation of the owners. Among the 16384 points of one device at most 192 have the same point_local // 8, and some value of it is taken by exactly 192 of them.
All inputs are finite; a program needn't handle non-finite values.
Results may differ from a plain program's by a relative error of at most 0.001.
Values may be sent and summed in bfloat16 or wider, within the bound.
No kernel may reach another device: no remote copies, remote signals or barrier semaphores. Data moves between devices by JAX's collectives and lax.ppermute only.
A program may use at most 128 MiB of HBM per device.

v0:
```python
import jax
import jax.numpy as jnp
import numpy as np
from jax import lax
from jax.sharding import PartitionSpec as P

NODES = 8


def gll_nodes(count):
    order = count - 1
    points = np.cos(np.pi * np.arange(count) / order)
    for sweep in range(100):
        oldest = np.ones(count)
        recent = points * 1.0
        for degree in range(2, order + 1):
            newest = ((2 * degree - 1) * points * recent - (degree - 1) * oldest) / degree
            oldest = recent
            recent = newest
        points = points - (points * recent - oldest) / (count * recent)
    return points[::-1]


def lagrange(coords, nodes):
    count = nodes.shape[0]
    result = []
    for i in range(count):
        term = jnp.ones_like(coords)
        for j in range(count):
            if j != i:
                term = term * ((coords - float(nodes[j])) * float(1.0 / (nodes[i] - nodes[j])))
        result.append(term)
    return jnp.stack(result, 0)


def evaluate(element_rows, basis):
    count = basis.shape[1]
    block = basis.shape[2]
    first, second, third = (basis[0], basis[1], basis[2])
    tensor = (first[:, None, None, :] * second[None, :, None, :] * third[None, None, :, :]).reshape(
        count**3, block
    )
    values = element_rows.reshape(block, -1, count**3).astype(jnp.float32)
    return jnp.sum(values * tensor.T[:, None, :], axis=2).T


def shards(file_fields, span_map, point_dest, point_local, point_coords):
    owners = lax.axis_size("owner")
    halves = lax.axis_size("sub")
    devices = owners * halves
    row_width = file_fields.shape[1]
    per_span = file_fields.shape[0] // devices
    nodes = gll_nodes(NODES)
    count_nodes = nodes.shape[0]
    fields = row_width // count_nodes**3
    columns = jnp.arange(devices, dtype=jnp.int32)
    inverse = jnp.zeros((devices,), jnp.int32).at[span_map[0]].set(columns)
    pieces = file_fields.reshape(devices, per_span, row_width)[inverse]
    owned = lax.all_to_all(pieces, ("owner", "sub"), split_axis=0, concat_axis=0, tiled=True)
    owned = owned.reshape(devices * per_span, row_width)
    destination = point_dest[:, 0]
    npoints = destination.shape[0]
    capacity = 2 * npoints // devices
    element_table = owned
    matches = (destination[:, None] == columns[None, :]).astype(jnp.int32)
    counts = jnp.sum(matches, axis=0)
    starts = jnp.cumsum(counts) - counts
    ordering = jnp.argsort(destination, stable=True)
    sorted_target = destination[ordering]
    sorted_pos = jnp.arange(npoints, dtype=jnp.int32) - starts[sorted_target]
    position = jnp.zeros((npoints,), jnp.int32).at[ordering].set(sorted_pos)
    id_buffer = (
        jnp.zeros((1, devices, capacity), jnp.int32).at[0, destination, position].set(point_local)
    )
    slots = devices * capacity
    coord_buffer = (
        jnp.zeros((3, devices, capacity), jnp.float32)
        .at[:, destination, position]
        .set(point_coords)
    )
    got_ids, got_data = (
        lax.all_to_all(id_buffer, ("owner", "sub"), split_axis=1, concat_axis=1, tiled=True),
        lax.all_to_all(coord_buffer, ("owner", "sub"), split_axis=1, concat_axis=1, tiled=True),
    )
    recv_basis = jnp.moveaxis(lagrange(got_data.reshape(3, slots), nodes), 0, 1)
    block = min(1024, slots)
    number = slots // block
    id_blocks = got_ids.reshape(number, block)
    basis_blocks = recv_basis.reshape(3, count_nodes, number, block).transpose(2, 0, 1, 3)
    computed = lax.map(
        lambda item: evaluate(element_table[item[0]], item[1]), (id_blocks, basis_blocks)
    )
    computed = computed.transpose(1, 0, 2).reshape(fields, devices, capacity)
    returned = lax.all_to_all(computed, ("owner", "sub"), split_axis=1, concat_axis=1, tiled=True)
    return (returned[:, destination, position], owned)


def solution(mesh):
    return jax.shard_map(
        shards,
        mesh=mesh,
        in_specs=(
            P(("owner", "sub"), None),
            P(("owner", "sub"), None),
            P(("owner", "sub"), None),
            P(("owner", "sub")),
            P(None, ("owner", "sub")),
        ),
        out_specs=(P(None, ("owner", "sub")), P(("owner", "sub"), None)),
        check_vma=False,
    )
```

profile of v0, /device:TPU:1, one launch (start us, length us, event | category | flops | bytes accessed | tf_op | source)
XLA Modules:
  0.0 1720.1 jit_solution(5683057078421198564)
XLA Ops:
  8.4 8.6 sort.17
  17.0 90.5 %gather_fusion.1 = s32[16384]{0:T(1024)S(1)} fusion(s32[16384]{0:T(1024)S(1)} %bitcast.58, s32[16384]{0:T(1024)S(1)} %get-tuple-element.95), kind=kCustom, calls=%fused_computation.1 | custom fusion | bytes 196608 | tf_op jit(solution)/shard_map/gather | solution.py:69
  107.7 97.2 %gather_fusion.2 = s32[16384]{0:T(1024)S(1)} fusion(s32[128]{0:T(128)S(1)} %sub.20, s32[16384]{0:T(1024)S(1)} %broadcast_clamp_fusion.1), kind=kCustom, calls=%fused_computation.2 | custom fusion | bytes 196608 | tf_op jit(solution)/shard_map/gather | solution.py:70
  204.9 60.3 %scatter_custom_fusion = s32[16384]{0:T(1024)S(1)} fusion(s32[16384]{0:T(1024)S(1)} %get-tuple-element.96, s32[16384]{0:T(1024)S(1)} %iota_subtract_fusion, s32[]{:T(128)} %constant.55.clone.1), kind=kCustom, calls=%fused_computation.51 | custom fusion | bytes 65540 | tf_op jit(solution)/shard_map/scatter | solution.py:71
  266.3 61.2 %scatter_custom_fusion.2 = s32[32768]{0:T(1024)} fusion(s32[16384]{0:T(1024)S(1)} %broadcast_select_fusion.1, s32[16384]{0:T(1024)} %param.10, s32[]{:T(128)} %constant.55.clone.1), kind=kCustom, calls=%fused_computation.44 | custom fusion | bytes 131584
  327.5 11.5 all-to-all-start
  344.7 47.4 %scatter_custom_fusion.3 = f32[3,32768]{0,1:T(8,128)} fusion(s32[16384]{0:T(1024)S(1)} %broadcast_select_fusion, f32[16384,3]{1,0:T(8,128)} %copy.50, f32[]{:T(128)} %constant.56.clone.1), kind=kCustom, calls=%fused_computation.21 | custom fusion | bytes 393728
  392.1 9.9 copy.51
  402.0 9.8 all-to-all-start.2
  450.6 44.2 %all-to-all-done.1 = bf16[128,8,2560]{2,1,0:T(8,128)(2,1)} async-done(((bf16[128,8,2560]{2,1,0:T(8,128)(2,1)}), bf16[128,8,2560]{2,1,0:T(8,128)(2,1)}, u32[]{:S(2)}, u32[]{:S(2)}) %all-to-all-start.1) | async-done | bytes 5242912 | tf_op jit(solution)/shard_map/all_to_all | solution.py:59
  494.8 945.0 %while.10 = (s32[]{:T(128)}, f32[32,5,1024]{2,1,0:T(8,128)}, s32[32,1024]{1,0:T(8,128)S(1)}, bf16[1024,2560]{1,0:T(8,128)(2,1)}, f32[32,3,8,1024]{3,0,1,2:T(8,128)}, /*index=5*/s32[]{:T(128)}, s32[]{:T(128)}, s32[]{}, s32[]{}) while((s32[]{:T(128)}, f32[32,5,1024]{2,1,0:T(8,128)}, s32[32,1024]{1,0:T(8,128)S(1)}, ...), condition=%wide.region_9.10_spmd, body=%wide.region_7.9_spmd.sunk | while | flops 5831684 | bytes 42005124 | solution.py:90
  496.3 13.6 gather_fusion
  509.9 8.2 copy.79
  525.8 13.6 gather_fusion
  555.4 13.6 gather_fusion
  569.0 8.2 copy.79
  584.9 13.6 gather_fusion
  614.4 13.6 gather_fusion
  644.0 13.6 gather_fusion
  673.5 13.6 gather_fusion
  703.0 13.6 gather_fusion
  732.6 13.6 gather_fusion
  762.1 13.6 gather_fusion
  791.6 13.6 gather_fusion
  821.2 13.6 gather_fusion
  850.7 13.6 gather_fusion
  880.2 13.6 gather_fusion
  909.7 13.6 gather_fusion
  939.3 13.6 gather_fusion
  968.8 13.6 gather_fusion
  998.3 13.6 gather_fusion
  1027.9 13.6 gather_fusion
  1057.4 13.6 gather_fusion
  1086.9 13.6 gather_fusion
  1116.5 13.6 gather_fusion
  1146.0 13.6 gather_fusion
  1175.5 13.6 gather_fusion
  1205.1 13.6 gather_fusion
  1234.6 13.6 gather_fusion
  1264.1 13.6 gather_fusion
  1293.6 13.6 gather_fusion
  1323.2 13.6 gather_fusion
  1352.7 13.6 gather_fusion
  1382.2 13.6 gather_fusion
  1411.8 13.6 gather_fusion
  1439.8 24.2 %all_to_all.20 = f32[5,128,256]{2,0,1:T(8,128)S(1)} all-to-all(f32[5,128,256]{2,0,1:T(8,128)} %bitcast.72), channel_id=1, replica_groups=mesh['owner'=64,'sub'=2] {'owner','sub'}, dimensions={1} | all-to-all | bytes 1310720 | tf_op jit(solution)/shard_map/all_to_all | solution.py:94
  1464.0 8.3 copy.62
  1472.3 236.6 %gather_fusion.4 = f32[16384,5]{1,0:T(8,128)} fusion(f32[5,128,256]{0,2,1:T(8,128)} %copy.62, s32[16384]{0:T(1024)S(1)} %bitcast.59), kind=kCustom, calls=%fused_computation.4 | custom fusion | bytes 786432 | tf_op jit(solution)/shard_map/gather | solution.py:95
  (387 shorter events, 556.5 us)
Async XLA Ops:
  0.6 16.4 copy-start
  107.7 157.9 %copy-start.6 = (s32[3]{0:T(128)S(1)}, s32[3]{0:T(128)}, u32[]{:S(2)}) copy-start(s32[3]{0:T(128)} %constant.124) | copy-start | bytes 40
  107.7 158.3 %copy-start.5 = (s32[3]{0:T(128)S(1)}, s32[3]{0:T(128)}, u32[]{:S(2)}) copy-start(s32[3]{0:T(128)} %constant.127) | copy-start | bytes 40
  107.7 231.3 %copy-start.4 = (s32[2]{0:T(128)S(1)}, s32[2]{0:T(128)}, u32[]{:S(2)}) copy-start(s32[2]{0:T(128)} %constant.130) | copy-start | bytes 28
  107.7 231.6 %copy-start.3 = (s32[2]{0:T(128)S(1)}, s32[2]{0:T(128)}, u32[]{:S(2)}) copy-start(s32[2]{0:T(128)} %constant.133) | copy-start | bytes 28
  107.7 231.9 %copy-start.2 = (f32[3,16384]{1,0:T(4,128)S(1)}, f32[3,16384]{1,0:T(4,128)}, u32[]{:S(2)}) copy-start(f32[3,16384]{1,0:T(4,128)} %param.11) | copy-start | bytes 589828
  327.5 74.5 %all-to-all-start = ((s32[1,128,256]{2,0,1:T(1,128)}), s32[1,128,256]{2,0,1:T(1,128)S(1)}, u32[]{:S(2)}, u32[]{:S(2)}) async-start(s32[1,128,256]{2,0,1:T(1,128)} %bitcast.17), calls=%async_computation | async-start | bytes 262144 | tf_op jit(solution)/shard_map/all_to_all | solution.py:82
  392.1 19.7 %copy-start.7 = (s32[1,128]{1,0:T(1,128)S(1)}, s32[1,128]{1,0:T(1,128)}, u32[]{:S(2)}) copy-start(s32[1,128]{1,0:T(1,128)} %param.8) | copy-start | bytes 1540
  402.0 23.5 %all-to-all-start.2 = ((f32[3,128,256]{2,0,1:T(4,128)}), f32[3,128,256]{2,0,1:T(4,128)S(1)}, u32[]{:S(2)}, u32[]{:S(2)}) async-start(f32[3,128,256]{2,0,1:T(4,128)} %copy.51), calls=%async_computation.2 | async-start | bytes 1048576 | tf_op jit(solution)/shard_map/all_to_all | solution.py:83
  425.5 69.3 %all-to-all-start.1 = ((bf16[128,8,2560]{2,1,0:T(8,128)(2,1)}), bf16[128,8,2560]{2,1,0:T(8,128)(2,1)}, u32[]{:S(2)}, u32[]{:S(2)}) async-start(bf16[128,8,2560]{2,1,0:T(8,128)(2,1)} %gather_fusion.3), calls=%async_computation.1 | async-start | bytes 10485760 | tf_op jit(solution)/shard_map/all_to_all | solution.py:59
  439.4 4.5 copy-start.1
where the time goes:
time: 1730 us; the launch traced here: 1720 us
  local copies, waits for them, and re-layouts  1410 us (82%)
  other arithmetic  209 us (12%)
  waiting for transfers between devices  50.8 us (3%)
  starting transfers between devices  26.7 us (2%)
  blocking collectives  24.2 us (1%)
    gather x32, local copies, waits for them, and re-layouts, shards(): element_table[item[0]]  435 us
    convert_element_type x32, local copies, waits for them, and re-layouts, evaluate(): values = element_rows.reshape(block, -1, count ** 3).astype(jnp.float32)  263 us
    gather x1, local copies, waits for them, and re-layouts, shards(): return (returned[:, destination, position], owned)  237 us
    reduce_sum x32, other arithmetic, evaluate(): return jnp.sum(values * tensor.T[:, None, :], axis=2).T  178 us
    unnamed x28, local copies, waits for them, and re-layouts  131 us
    gather x1, local copies, waits for them, and re-layouts, shards(): sorted_pos = jnp.arange(npoints, dtype=jnp.int32) - starts[sorted_target]  97.2 us
    gather x1, local copies, waits for them, and re-layouts, shards(): sorted_target = destination[ordering]  90.5 us
    scatter x1, local copies, waits for them, and re-layouts, shards(): position = jnp.zeros((npoints,), jnp.int32).at[ordering].set(sorted_pos)  60.3 us
  transfers between devices with their start and end apart: 3, of which 2 were waited for; matrix products, arithmetic and copies ran while one was open for 5% of the time, Pallas kernels for 0%

commit v1 on v0

v1 whole, which is shorter than its diff:
```python
import jax
import jax.numpy as jnp
import numpy as np
from jax import lax
from jax.experimental import pallas as pl
from jax.experimental.pallas import tpu as pltpu
from jax.sharding import PartitionSpec as P

NODES = 8
FIELDS = 5
SPAN = 8
DEVICES = 128
POINTS = 16384
CAP = 192
HALF = 64
WIDTH = FIELDS * NODES**3
SLOTS = DEVICES * CAP
GROUP = 64
GROUPS = 16
TILE = 256
AXES = ("owner", "sub")
F32 = jnp.float32
BF16 = jnp.bfloat16
I32 = jnp.int32


def gll_nodes(count):
    order = count - 1
    points = np.cos(np.pi * np.arange(count) / order)
    for sweep in range(100):
        oldest = np.ones(count)
        recent = points * 1.0
        for degree in range(2, order + 1):
            newest = ((2 * degree - 1) * points * recent - (degree - 1) * oldest) / degree
            oldest = recent
            recent = newest
        points = points - (points * recent - oldest) / (count * recent)
    return points[::-1]


def iota(shape, dim):
    return lax.broadcasted_iota(I32, shape, dim)


def lane_dot(a, b):
    return lax.dot_general(a, b, (((1,), (1,)), ((), ())), preferred_element_type=F32)


def dot(a, b):
    return jnp.dot(a, b, preferred_element_type=F32)


def parts(x):
    high = x.astype(BF16).astype(F32)
    return high, x - high


def earlier(rows, cols):
    return jnp.where(iota((rows, cols), 0) < iota((rows, cols), 1), 1.0, 0.0).astype(BF16)


def ranks(mask, before, base):
    ones = jnp.where(mask, 1.0, 0.0)
    narrow = ones.astype(BF16)
    counts = []
    for j in range(mask.shape[1] // 256):
        part = slice(256 * j, 256 * j + 256)
        inside = dot(narrow[:, part], before)
        counts.append(inside + base)
        base = base + inside[:, 255:256] + ones[:, 256 * j + 255 : 256 * j + 256]
    count = jnp.concatenate(counts, axis=1)
    return jnp.sum(jnp.where(mask, count, 0.0), axis=0, keepdims=True), base


def spread(mask, value):
    return jnp.where(mask, value, 0.0).astype(BF16)


A_LANES = 1024


def bucket_kernel(dest_ref, local_ref, coords_ref, out_ref, pos_ref, acc_ref):
    acc_ref[...] = jnp.zeros_like(acc_ref)
    before = earlier(256, 256)

    def step(n, base):
        lanes = pl.ds(pl.multiple_of(n * A_LANES, A_LANES), A_LANES)
        local = local_ref[:, lanes]
        mask = iota((DEVICES, A_LANES), 0) == (local >> 3)
        pos, base = ranks(mask, before, base)
        pos = pos.astype(I32)
        pos_ref[:, lanes] = pos
        place = jnp.where(iota((256, A_LANES), 0) == pos, 1.0, 0.0).astype(BF16)
        wide = jnp.concatenate([place, place], axis=1)
        rows = []
        for k in range(3):
            high, low = parts(coords_ref[k : k + 1, lanes])
            rows.append(jnp.concatenate([spread(mask, high), spread(mask, low)], axis=1))
        high = (dest_ref[:, lanes] * 8 + 8).astype(F32)
        low = (local & 7).astype(F32)
        rows.append(jnp.concatenate([spread(mask, high), spread(mask, low)], axis=1))
        acc_ref[...] += lane_dot(jnp.concatenate(rows, axis=0), wide)
        return base

    lax.fori_loop(0, POINTS // A_LANES, step, jnp.zeros((DEVICES, 1), F32))
    for k in range(4):
        out_ref[:, k, :] = acc_ref[k * 128 : k * 128 + 128, 0:128]
        out_ref[:, 4 + k, :] = acc_ref[k * 128 : k * 128 + 128, 128:256]


def bucket(dest, local, coords):
    return pl.pallas_call(
        bucket_kernel,
        out_shape=(
            jax.ShapeDtypeStruct((DEVICES, 8, 128), F32),
            jax.ShapeDtypeStruct((1, POINTS), I32),
        ),
        in_specs=[pl.BlockSpec(memory_space=pltpu.VMEM)] * 3,
        out_specs=(pl.BlockSpec(memory_space=pltpu.VMEM),) * 2,
        scratch_shapes=[pltpu.VMEM((512, 256), F32)],
        compiler_params=pltpu.CompilerParams(vmem_limit_bytes=48 * 1024 * 1024),
        name="bucket",
    )(dest, local, coords)


SOURCES = 8
C_LANES = SOURCES * CAP
STEPS = DEVICES // SOURCES


def basis_rows(x, nodes, scale):
    row = iota((8, x.shape[1]), 0)
    out = None
    for n in range(8):
        term = jnp.where(row == n, scale, x - float(nodes[n]))
        out = term if out is None else out * term
    return out


def evaluate_kernel(
    recv_ref, span_ref, file_ref, out_ref, flat_ref, sorted_ref, slot_ref, val_ref, acc_ref, first_ref
):
    nodes = gll_nodes(NODES)
    before = earlier(256, 256)
    inverse = jnp.sum(
        jnp.where(iota((128, 128), 0) == span_ref[...], iota((128, 128), 1), 0).astype(F32),
        axis=1,
        keepdims=True,
    )
    lane = iota((8, 128), 1)

    def count(n, base):
        source = n * SOURCES
        blocks = [recv_ref[source + s] for s in range(SOURCES)]
        pairs = [
            jnp.where(lane < HALF, blocks[2 * s], pltpu.roll(blocks[2 * s + 1], HALF, 1))
            for s in range(SOURCES // 2)
        ]
        full = jnp.concatenate(blocks, axis=1)[0:4]
        rest = jnp.concatenate(pairs, axis=1)[4:8]
        data = jnp.concatenate([full, rest], axis=1)
        number = data[3:4].astype(I32)
        mask = iota((128, C_LANES), 0) == (number >> 3) - 1
        span = jnp.sum(jnp.where(mask, inverse, 0.0), axis=0, keepdims=True).astype(I32)
        group = jnp.where(number > 0, span >> 3, GROUPS)
        element = (span & 7) * 8 + (number & 7)
        rank, base = ranks(iota((GROUPS, C_LANES), 0) == group, before, base)
        lanes = pl.ds(pl.multiple_of(n * C_LANES, C_LANES), C_LANES)
        flat_ref[0:3, lanes] = data[0:3]
        flat_ref[3:4, lanes] = element.astype(F32)
        flat_ref[4:5, lanes] = group.astype(F32)
        flat_ref[5:6, lanes] = rank
        return base

    total = lax.fori_loop(0, STEPS, count, jnp.zeros((GROUPS, 1), F32))
    tiles = ((total.astype(I32) + (TILE - 1)) >> 8).astype(F32)
    lower = jnp.where(iota((GROUPS, GROUPS), 1) < iota((GROUPS, GROUPS), 0), 1.0, 0.0)
    start = dot(lower.astype(BF16), jnp.broadcast_to(tiles, (GROUPS, 128)).astype(BF16))[:, 0:1]
    for g in range(GROUPS):
        first_ref[g] = jnp.sum(start[g : g + 1]).astype(I32)
    first_ref[GROUPS] = jnp.sum(tiles).astype(I32)

    sorted_ref[...] = jnp.zeros_like(sorted_ref)
    slot_ref[...] = jnp.zeros_like(slot_ref)

    def sort(n, carry):
        lanes = pl.ds(pl.multiple_of(n * C_LANES, C_LANES), C_LANES)
        group = flat_ref[4:5, lanes].astype(I32)
        here = iota((GROUPS, C_LANES), 0) == group
        base = jnp.sum(jnp.where(here, start, 0.0), axis=0, keepdims=True)
        slot = base.astype(I32) * TILE + flat_ref[5:6, lanes].astype(I32)
        high = jnp.where(group < GROUPS, slot >> 8, -1)
        mask = iota((128, C_LANES), 0) == high
        place = jnp.where(iota((TILE, C_LANES), 0) == (slot & 255), 1.0, 0.0).astype(BF16)
        at = iota((1, C_LANES), 1)
        late = at - SOURCES * 128
        second = late >= 0
        source = n * SOURCES + jnp.where(second, late >> 6, at >> 7)
        column = jnp.where(second, 128 + (late & 63), at & 127).astype(F32)
        rows = []
        for k in range(3):
            top, low = parts(flat_ref[k : k + 1, lanes])
            rows.append(jnp.concatenate([spread(mask, top), spread(mask, low)], axis=1))
        top = ((source + 1) * 64).astype(F32)
        rows.append(
            jnp.concatenate([spread(mask, top), spread(mask, flat_ref[3:4, lanes])], axis=1)
        )
        wide = jnp.concatenate([place, place], axis=1)
        sorted_ref[...] += lane_dot(jnp.concatenate(rows, axis=0), wide)
        slot_ref[...] += lane_dot(spread(mask, column), place)
        return carry

    lax.fori_loop(0, STEPS, sort, 0)

    val_ref[...] = jnp.zeros_like(val_ref)
    scale = []
    for i in range(8):
        value = 1.0
        for n in range(8):
            if n != i:
                value = value / (nodes[i] - nodes[n])
        scale.append(float(value))
    row8 = iota((8, TILE), 0)
    scales = jnp.zeros((8, TILE), F32)
    for i in range(8):
        scales = jnp.where(row8 == i, scale[i], scales)

    def on_group(g, carry):
        rows = pl.ds(pl.multiple_of(g * GROUP, GROUP), GROUP)
        table = jnp.concatenate(
            [file_ref[rows, f * 512 : f * 512 + 512] for f in range(FIELDS)], axis=0
        )
        table = jnp.concatenate([table, table], axis=1)

        def on_tile(t, inner):
            b0 = basis_rows(sorted_ref[pl.ds(t, 1), :], nodes, scales)
            b1 = basis_rows(sorted_ref[pl.ds(128 + t, 1), :], nodes, scales)
            b2 = basis_rows(sorted_ref[pl.ds(256 + t, 1), :], nodes, scales)
            element = sorted_ref[pl.ds(384 + t, 1), :].astype(I32) & 63
            planes = jnp.concatenate([b1[j : j + 1] * b2 for j in range(8)], axis=0)
            tops, lows = [], []
            for i in range(8):
                tensor = b0[i : i + 1] * planes
                top = tensor.astype(BF16)
                tops.append(top)
                lows.append((tensor - top.astype(F32)).astype(BF16))
            result = dot(table, jnp.concatenate(tops + lows, axis=0))
            mask = iota((GROUP, TILE), 0) == element
            for f in range(FIELDS):
                part = result[f * GROUP : f * GROUP + GROUP]
                val_ref[pl.ds(f * 128 + t, 1), :] = jnp.sum(
                    jnp.where(mask, part, 0.0), axis=0, keepdims=True
                )
            return inner

        return lax.fori_loop(first_ref[g], first_ref[g + 1], on_tile, carry)

    lax.fori_loop(0, GROUPS, on_group, 0)

    acc_ref[...] = jnp.zeros_like(acc_ref)
    many = 4

    def back(n, carry):
        def row(ref, at):
            lines = [ref[pl.ds(at + n * many + q, 1), :] for q in range(many)]
            return jnp.concatenate(lines, axis=1)

        source = (row(sorted_ref, 384).astype(I32) >> 6) - 1
        column = row(slot_ref, 0).astype(I32)
        mask = iota((128, many * TILE), 0) == source
        place = jnp.where(iota((256, many * TILE), 0) == column, 1.0, 0.0).astype(BF16)
        wide = jnp.concatenate([place, place], axis=1)
        rows = []
        for f in range(FIELDS):
            top, low = parts(row(val_ref, f * 128))
            rows.append(jnp.concatenate([spread(mask, top), spread(mask, low)], axis=1))
        acc_ref[...] += lane_dot(jnp.concatenate(rows, axis=0), wide)
        return carry

    lax.fori_loop(0, (first_ref[GROUPS] + many - 1) // many, back, 0)
    late = []
    for f in range(FIELDS):
        out_ref[:, f, :] = acc_ref[f * 128 : f * 128 + 128, 0:128]
        late.append(acc_ref[f * 128 : f * 128 + 128, 128:256])
    late.append(jnp.zeros_like(late[0]))
    low = iota((128, 128), 1) < HALF
    for f in range(3):
        out_ref[:, FIELDS + f, :] = jnp.where(low, late[2 * f], pltpu.roll(late[2 * f + 1], HALF, 1))


def evaluate(recv, span, file_fields):
    return pl.pallas_call(
        evaluate_kernel,
        out_shape=jax.ShapeDtypeStruct((DEVICES, 8, 128), F32),
        in_specs=[pl.BlockSpec(memory_space=pltpu.VMEM)] * 3,
        out_specs=pl.BlockSpec(memory_space=pltpu.VMEM),
        scratch_shapes=[
            pltpu.VMEM((8, SLOTS), F32),
            pltpu.VMEM((512, TILE), F32),
            pltpu.VMEM((128, TILE), F32),
            pltpu.VMEM((FIELDS * 128, TILE), F32),
            pltpu.VMEM((FIELDS * 128, 256), F32),
            pltpu.SMEM((GROUPS + 1,), I32),
        ],
        compiler_params=pltpu.CompilerParams(vmem_limit_bytes=56 * 1024 * 1024),
        cost_estimate=pl.CostEstimate(
            flops=60_000_000_000, bytes_accessed=6_000_000, transcendentals=0
        ),
        name="evaluate",
    )(recv, span, file_fields)


E_LANES = 256


def collect_kernel(back_ref, local_ref, pos_ref, out_ref, table_ref):
    for f in range(FIELDS):
        first = back_ref[:, f, :]
        second = back_ref[:, FIELDS + f // 2, :]
        if f % 2:
            second = pltpu.roll(second, HALF, 1)
        high, low = parts(jnp.concatenate([first, second], axis=1))
        table_ref[f * 128 : f * 128 + 128, 0:256] = high.astype(BF16)
        table_ref[f * 128 : f * 128 + 128, 256:512] = low.astype(BF16)

    def step(n, carry):
        lanes = pl.ds(pl.multiple_of(n * E_LANES, E_LANES), E_LANES)
        mask = iota((128, E_LANES), 0) == (local_ref[:, lanes] >> 3)
        place = jnp.where(iota((256, E_LANES), 0) == pos_ref[:, lanes], 1.0, 0.0).astype(BF16)
        got = dot(table_ref[...], jnp.concatenate([place, place], axis=0))
        for f in range(FIELDS):
            out_ref[f : f + 1, lanes] = jnp.sum(
                jnp.where(mask, got[f * 128 : f * 128 + 128], 0.0), axis=0, keepdims=True
            )
        return carry

    lax.fori_loop(0, POINTS // E_LANES, step, 0)


def collect(back, local, pos):
    return pl.pallas_call(
        collect_kernel,
        out_shape=jax.ShapeDtypeStruct((FIELDS, POINTS), F32),
        in_specs=[pl.BlockSpec(memory_space=pltpu.VMEM)] * 3,
        out_specs=pl.BlockSpec(memory_space=pltpu.VMEM),
        scratch_shapes=[pltpu.VMEM((FIELDS * 128, 512), BF16)],
        compiler_params=pltpu.CompilerParams(vmem_limit_bytes=48 * 1024 * 1024),
        name="collect",
    )(back, local, pos)


def exchange(x):
    return lax.all_to_all(x, AXES, split_axis=0, concat_axis=0, tiled=True)


def shards(file_fields, span_map, point_dest, point_local, point_coords):
    columns = jnp.arange(DEVICES, dtype=I32)
    inverse = jnp.zeros((DEVICES,), I32).at[span_map[0]].set(columns)
    pieces = file_fields.reshape(DEVICES, SPAN, WIDTH)[inverse]
    local = point_local.reshape(1, POINTS)
    sent, pos = bucket(point_dest.reshape(1, POINTS), local, point_coords)
    recv = exchange(sent)
    pieces, recv = lax.optimization_barrier((pieces, recv))
    owned = exchange(pieces).reshape(DEVICES * SPAN, WIDTH)
    values = evaluate(recv, span_map, file_fields)
    back = exchange(values)
    return collect(back, local, pos), owned


def solution(mesh):
    return jax.shard_map(
        shards,
        mesh=mesh,
        in_specs=(
            P(AXES, None),
            P(AXES, None),
            P(AXES, None),
            P(AXES),
            P(None, AXES),
        ),
        out_specs=(P(None, AXES), P(AXES, None)),
        check_vma=False,
    )
```

time: 1730 us -> 219 us (0.13)
  local copies, waits for them, and re-layouts: 1410 us -> 15.3 us
  other arithmetic: 209 us -> 0.67 us
  Pallas kernels: 0 us -> 115 us
    gather x36 -> x1, local copies, waits for them, and re-layouts: 865 us -> 5.73 us  [shards(): pieces = file_fields.reshape(DEVICES, SPAN, WIDTH)[inverse]]
    convert_element_type x32 -> x0, local copies, waits for them, and re-layouts: 263 us -> none  [evaluate(): values = element_rows.reshape(block, -1, count ** 3).astype(jnp.float32)]
    reduce_sum x33 -> x0, other arithmetic: 185 us -> none  [the longest x32 178 us: evaluate(): return jnp.sum(values * tensor.T[:, None, :], axis=2).T]
    unnamed x28 -> x11, local copies, waits for them, and re-layouts: 131 us -> 8.6 us
    pallas_call x0 -> x3, Pallas kernels: none -> 115 us  [the longest x1 75.4 us: evaluate(): pl.pallas_call(evaluate_kernel, out_shape=jax.ShapeDtypeStruct((DEVICES,...]
    scatter x3 -> x1, local copies, waits for them, and re-layouts: 71.2 us -> 0.97 us  [shards(): inverse = jnp.zeros((DEVICES,), I32).at[span_map[0]].set(columns)]
    slice x32 -> x0, local copies, waits for them, and re-layouts: 37.8 us -> none  [evaluate(): first, second, third = (basis[0], basis[1], basis[2])]
    dynamic_update_slice x32 -> x0, local copies, waits for them, and re-layouts: 19.5 us -> none  [shards(): lax.map(lambda item: evaluate(element_table[item[0]], item[1]), (id_block...]
  transfers between devices with their start and end apart: 3 -> 2, of which waited for: 2 -> 2; matrix products, arithmetic and copies ran while one was open for 5% -> 3% of each run, Pallas kernels for 0% -> 11%
where the time goes in v1:
time: 219 us
  Pallas kernels  115 us (53%)
  waiting for transfers between devices  46.8 us (21%)
  blocking collectives  22.9 us (10%)
  starting transfers between devices  17 us (8%)
  local copies, waits for them, and re-layouts  15.3 us (7%)
    pallas_call x1, Pallas kernels, evaluate(): pl.pallas_call(evaluate_kernel, out_shape=jax.ShapeDtypeStruct((DEVICES,...  75.4 us
    all_to_all x2, waiting for transfers between devices, exchange(): return lax.all_to_all(x, AXES, split_axis=0, concat_axis=0, tiled=True)  46.8 us
    pallas_call x1, Pallas kernels, collect(): pl.pallas_call(collect_kernel, out_shape=jax.ShapeDtypeStruct((FIELDS, PO...  23.4 us
    all_to_all x1, blocking collectives, exchange(): return lax.all_to_all(x, AXES, split_axis=0, concat_axis=0, tiled=True)  22.9 us
    all_to_all x2, starting transfers between devices, exchange(): return lax.all_to_all(x, AXES, split_axis=0, concat_axis=0, tiled=True)  17 us
    pallas_call x1, Pallas kernels, bucket(): pl.pallas_call(bucket_kernel, out_shape=(jax.ShapeDtypeStruct((DEVICES, 8...  16.7 us
    unnamed x11, local copies, waits for them, and re-layouts  8.6 us
    gather x1, local copies, waits for them, and re-layouts, shards(): pieces = file_fields.reshape(DEVICES, SPAN, WIDTH)[inverse]  5.73 us
  transfers between devices with their start and end apart: 2, of which 2 were waited for; matrix products, arithmetic and copies ran while one was open for 3% of the time, Pallas kernels for 11%

profile of v1, /device:TPU:1, one launch (start us, length us, event | category | flops | bytes accessed | tf_op | source)
XLA Modules:
  0.0 218.8 jit_solution(4435399863216851932)
XLA Ops:
  0.6 0.0 copy-start
  0.6 0.9 copy-done
  1.6 0.0 copy-start.1
  1.6 0.8 copy-done.1
  2.4 0.0 copy-start.3
  2.4 0.8 copy-done.3
  3.3 16.7 %bucket.1 = (f32[128,8,128]{2,1,0:T(8,128)}, s32[1,16384]{1,0:T(1,128)S(1)}) custom-call(s32[1,16384]{1,0:T(1,128)S(1)} %bitcast.11, s32[1,16384]{1,0:T(1,128)S(1)} %bitcast.9, f32[3,16384]{1,0:T(4,128)S(1)} %copy-done), custom_call_target="tpu_custom_call" | custom-call | tf_op jit(solution)/shard_map/bucket/pallas_call | solution.py:112
  20.0 11.5 %all-to-all-start = ((f32[128,8,128]{2,1,0:T(8,128)}), f32[128,8,128]{2,1,0:T(8,128)S(1)}, u32[]{:S(2)}, u32[]{:S(2)}) async-start(f32[128,8,128]{2,1,0:T(8,128)} %get-tuple-element.6), calls=%async_computation | async-start | bytes 1048576 | tf_op jit(solution)/shard_map/all_to_all | solution.py:353
  31.5 0.7 fusion
  32.2 1.0 scatter_custom_fusion
  33.2 5.7 %gather_fusion = bf16[128,8,2560]{2,1,0:T(8,128)(2,1)} fusion(bf16[128,8,2560]{2,1,0:T(8,128)(2,1)} %bitcast.12, s32[1024]{0:T(1024)S(1)} %pad_clamp_fusion), kind=kCustom, calls=%fused_computation | custom fusion | bytes 10486272 | tf_op jit(solution)/shard_map/gather | solution.py:359
  38.9 6.3 %all-to-all-done.recv_ref = f32[128,8,128]{2,1,0:T(8,128)S(1)} async-done(((f32[128,8,128]{2,1,0:T(8,128)}), f32[128,8,128]{2,1,0:T(8,128)S(1)}, u32[]{:S(2)}, u32[]{:S(2)}) %all-to-all-start) | async-done | bytes 524320 | tf_op jit(solution)/shard_map/all_to_all | solution.py:353
  45.2 0.0 copy-start.4
  45.2 0.8 copy-done.4
  46.0 75.4 %evaluate.1 = f32[128,8,128]{2,1,0:T(8,128)} custom-call(f32[128,8,128]{2,1,0:T(8,128)} %copy-done.4, s32[1,128]{1,0:T(1,128)} %span_ref.1, bf16[1024,2560]{1,0:T(8,128)(2,1)} %file_ref.1), custom_call_target="tpu_custom_call" | custom-call | flops 60000002048 | bytes 6000000 | tf_op jit(solution)/shard_map/evaluate/pallas_call | solution.py:292
  121.4 22.9 %all_to_all.15.back_ref = f32[128,8,128]{2,1,0:T(8,128)S(1)} all-to-all(f32[128,8,128]{2,1,0:T(8,128)} %evaluate.1), channel_id=1, replica_groups=mesh['owner'=64,'sub'=2] {'owner','sub'}, dimensions={0} | all-to-all | bytes 1048576 | tf_op jit(solution)/shard_map/all_to_all | solution.py:353
  144.2 0.0 copy-start.2
  144.2 5.5 %all-to-all-start.2 = ((bf16[128,8,2560]{2,1,0:T(8,128)(2,1)}), bf16[128,8,2560]{2,1,0:T(8,128)(2,1)}, u32[]{:S(2)}, u32[]{:S(2)}) async-start(bf16[128,8,2560]{2,1,0:T(8,128)(2,1)} %gather_fusion), calls=%async_computation.2 | async-start | bytes 10485760 | tf_op jit(solution)/shard_map/all_to_all | solution.py:353
  149.8 0.0 copy-done.2
  149.8 23.4 %collect.1 = f32[5,16384]{1,0:T(8,128)} custom-call(f32[128,8,128]{2,1,0:T(8,128)S(1)} %all_to_all.15.back_ref, s32[1,16384]{1,0:T(1,128)S(1)} %bitcast.10, s32[1,16384]{1,0:T(1,128)S(1)} %get-tuple-element.8.pos_ref), custom_call_target="tpu_custom_call" | custom-call | tf_op jit(solution)/shard_map/collect/pallas_call | solution.py:341
  173.1 40.5 %all-to-all-done.2 = bf16[128,8,2560]{2,1,0:T(8,128)(2,1)} async-done(((bf16[128,8,2560]{2,1,0:T(8,128)(2,1)}), bf16[128,8,2560]{2,1,0:T(8,128)(2,1)}, u32[]{:S(2)}, u32[]{:S(2)}) %all-to-all-start.2) | async-done | bytes 5242912 | tf_op jit(solution)/shard_map/all_to_all | solution.py:353
  213.7 5.2 %copy.8 = bf16[1024,2560]{1,0:T(8,128)(2,1)} copy(bf16[1024,2560]{1,0:T(8,128)(2,1)} %bitcast.5) | data formatting | bytes 10485760
  (3 shorter events, 0.0 us)
Async XLA Ops:
  0.6 1.0 copy-start
  1.6 0.8 copy-start.1
  2.4 0.8 copy-start.3
  20.0 25.2 %all-to-all-start = ((f32[128,8,128]{2,1,0:T(8,128)}), f32[128,8,128]{2,1,0:T(8,128)S(1)}, u32[]{:S(2)}, u32[]{:S(2)}) async-start(f32[128,8,128]{2,1,0:T(8,128)} %get-tuple-element.6), calls=%async_computation | async-start | bytes 1048576 | tf_op jit(solution)/shard_map/all_to_all | solution.py:353
  45.2 0.8 copy-start.4
  144.2 5.5 %copy-start.2 = (s32[16384]{0:T(1024)S(1)}, s32[16384]{0:T(1024)}, u32[]{:S(2)}) copy-start(s32[16384]{0:T(1024)} %param.8) | copy-start | bytes 196612
  144.2 69.4 %all-to-all-start.2 = ((bf16[128,8,2560]{2,1,0:T(8,128)(2,1)}), bf16[128,8,2560]{2,1,0:T(8,128)(2,1)}, u32[]{:S(2)}, u32[]{:S(2)}) async-start(bf16[128,8,2560]{2,1,0:T(8,128)(2,1)} %gather_fusion), calls=%async_computation.2 | async-start | bytes 10485760 | tf_op jit(solution)/shard_map/all_to_all | solution.py:353

commit v2 on v1

v2 whole, which is shorter than its diff:
```python
import jax
import jax.numpy as jnp
import numpy as np
from jax import lax
from jax.experimental import pallas as pl
from jax.experimental.pallas import tpu as pltpu
from jax.sharding import PartitionSpec as P

NODES = 8
FIELDS = 5
SPAN = 8
DEVICES = 128
POINTS = 16384
CAP = 192
HALF = 64
WIDTH = FIELDS * NODES**3
SLOTS = DEVICES * CAP
GROUP = 64
GROUPS = 16
TILE = 256
ROWS = SLOTS // 256
MOST = SLOTS // TILE + GROUPS
AXES = ("owner", "sub")
F32 = jnp.float32
BF16 = jnp.bfloat16
I32 = jnp.int32


def gll_nodes(count):
    order = count - 1
    points = np.cos(np.pi * np.arange(count) / order)
    for sweep in range(100):
        oldest = np.ones(count)
        recent = points * 1.0
        for degree in range(2, order + 1):
            newest = ((2 * degree - 1) * points * recent - (degree - 1) * oldest) / degree
            oldest = recent
            recent = newest
        points = points - (points * recent - oldest) / (count * recent)
    return points[::-1]


def iota(shape, dim):
    return lax.broadcasted_iota(I32, shape, dim)


def lane_dot(a, b):
    return lax.dot_general(a, b, (((1,), (1,)), ((), ())), preferred_element_type=F32)


def dot(a, b):
    return jnp.dot(a, b, preferred_element_type=F32)


def parts(x):
    high = x.astype(BF16).astype(F32)
    return high, x - high


def earlier(rows, cols):
    return jnp.where(iota((rows, cols), 0) < iota((rows, cols), 1), 1.0, 0.0).astype(BF16)


def packed(value):
    return jnp.broadcast_to(value.astype(F32), (16, value.shape[1])).astype(BF16)


def onehot(first, rows, value):
    value = packed(value)
    base = iota(value.shape, 0)
    one, zero = jnp.asarray(1.0, BF16), jnp.asarray(0.0, BF16)
    out = []
    for r in range(rows // 16):
        out.append(jnp.where((base + (first + 16 * r)).astype(F32).astype(BF16) == value, one, zero))
    return jnp.concatenate(out, axis=0)


def spread(ones, value):
    value = packed(value)
    return jnp.concatenate(
        [ones[16 * r : 16 * r + 16] * value for r in range(ones.shape[0] // 16)], axis=0
    )


def both(ones, high, low):
    return jnp.concatenate([spread(ones, high), spread(ones, low)], axis=1)


def ranks(mask, before, base):
    ones = jnp.where(mask, 1.0, 0.0)
    narrow = ones.astype(BF16)
    counts = []
    for j in range(mask.shape[1] // 256):
        part = slice(256 * j, 256 * j + 256)
        inside = dot(narrow[:, part], before)
        counts.append(inside + base)
        base = base + inside[:, 255:256] + ones[:, 256 * j + 255 : 256 * j + 256]
    count = jnp.concatenate(counts, axis=1)
    return jnp.sum(jnp.where(mask, count, 0.0), axis=0, keepdims=True), base


def flat_slot(block, place):
    odd = (block & 1) == 1
    late = place >= 128
    return block * CAP + jnp.where(odd, jnp.where(late, place - 128, place + 64), place)


A_LANES = 2048


def bucket_kernel(
    dest_hbm, local_hbm, coords_hbm, out_ref, slot_ref, dest_ref, local_ref, coords_ref, acc_ref, flat_ref, sems
):
    copies = [
        pltpu.make_async_copy(src, dst, sems.at[n])
        for n, (src, dst) in enumerate(
            [(local_hbm, local_ref), (dest_hbm, dest_ref), (coords_hbm, coords_ref)]
        )
    ]
    for copy in copies:
        copy.start()
    acc_ref[...] = jnp.zeros_like(acc_ref)
    before = earlier(256, 256)
    steps = POINTS // A_LANES

    def at(n):
        return pl.ds(pl.multiple_of(n * A_LANES, A_LANES), A_LANES)

    def place(n, base):
        holder = local_ref[:, at(n)] >> 3
        rank, base = ranks(iota((DEVICES, A_LANES), 0) == holder, before, base)
        slot_ref[:, at(n)] = flat_slot(holder, rank.astype(I32))
        return base

    def scatter(n):
        slot = slot_ref[:, at(n)]
        where_row = onehot(0, ROWS, slot >> 8)
        where_col = onehot(0, 256, slot & 255)
        rows = [both(where_row, *parts(coords_ref[k : k + 1, at(n)])) for k in range(3)]
        rows.append(both(where_row, dest_ref[:, at(n)] * 8 + 8, local_ref[:, at(n)] & 7))
        wide = jnp.concatenate([where_col, where_col], axis=1)
        return lane_dot(jnp.concatenate(rows, axis=0), wide)

    copies[0].wait()
    base = place(0, jnp.zeros((DEVICES, 1), F32))
    copies[1].wait()
    copies[2].wait()

    def step(n, base):
        got = scatter(n)
        base = place(n + 1, base)
        acc_ref[...] += got
        return base

    lax.fori_loop(0, steps - 1, step, base)
    acc_ref[...] += scatter(steps - 1)
    for k in range(4):
        block = acc_ref[k * ROWS : k * ROWS + ROWS, :]
        flat_ref[pl.ds(0, ROWS, 2), :] = block[:, 0:128]
        flat_ref[pl.ds(1, ROWS, 2), :] = block[:, 128:256]
        out_ref[:, k, :] = flat_ref[pl.ds(0, 64, 3), :]
        out_ref[:, 8 + k, :] = flat_ref[pl.ds(2, 64, 3), :]
        middle = flat_ref[pl.ds(1, 64, 3), :]
        out_ref[:, 4 + k, :] = middle
        out_ref[:, 12 + k, :] = pltpu.roll(middle, HALF, 1)


def bucket(dest, local, coords):
    return pl.pallas_call(
        bucket_kernel,
        out_shape=(
            jax.ShapeDtypeStruct((DEVICES // 2, 16, 128), F32),
            jax.ShapeDtypeStruct((1, POINTS), I32),
        ),
        in_specs=[pl.BlockSpec(memory_space=pl.ANY)] * 3,
        out_specs=(pl.BlockSpec(memory_space=pltpu.VMEM),) * 2,
        scratch_shapes=[
            pltpu.VMEM((1, POINTS), I32),
            pltpu.VMEM((1, POINTS), I32),
            pltpu.VMEM((3, POINTS), F32),
            pltpu.VMEM((4 * ROWS, 256), F32),
            pltpu.VMEM((2 * ROWS, 128), F32),
            pltpu.SemaphoreType.DMA((3,)),
        ],
        compiler_params=pltpu.CompilerParams(vmem_limit_bytes=56 * 1024 * 1024),
        name="bucket",
    )(dest, local, coords)


SOURCES = 16
C_LANES = SOURCES * CAP
STEPS = DEVICES // SOURCES
USUAL = 96
PAIR = 2
MANY = 8


def basis_rows(x, nodes, scale):
    row = iota((8, x.shape[1]), 0)
    out = None
    for n in range(8):
        term = jnp.where(row == n, scale, x - float(nodes[n]))
        out = term if out is None else out * term
    return out


def evaluate_kernel(
    recv_ref, span_ref, file_hbm, out_ref, file_ref, data_ref, sorted_ref, val_ref, acc_ref, flat_ref, first_ref, group_ref, sem
):
    load = pltpu.make_async_copy(file_hbm, file_ref, sem)
    load.start()
    nodes = gll_nodes(NODES)
    before = earlier(256, 256)
    permutation = jnp.where(iota((128, 128), 0) == span_ref[...], 1.0, 0.0).astype(BF16)
    inverse = lane_dot(iota((16, 128), 1).astype(F32).astype(BF16), permutation).astype(BF16)
    lane = iota((8, 128), 1)

    def count(n, base):
        source = n * SOURCES
        blocks = [recv_ref[source + s] for s in range(SOURCES)]
        pairs = [
            jnp.where(lane < HALF, blocks[2 * s], pltpu.roll(blocks[2 * s + 1], HALF, 1))
            for s in range(SOURCES // 2)
        ]
        full = jnp.concatenate(blocks, axis=1)[0:4]
        rest = jnp.concatenate(pairs, axis=1)[4:8]
        data = jnp.concatenate([full, rest], axis=1)
        number = data[3:4].astype(I32)
        span = dot(inverse, onehot(0, 128, (number >> 3) - 1))[0:1].astype(I32)
        group = jnp.where(number > 0, span >> 3, GROUPS)
        element = (span & 7) * 8 + (number & 7)
        rank, base = ranks(iota((GROUPS, C_LANES), 0) == group, before, base)
        lanes = pl.ds(pl.multiple_of(n * C_LANES, C_LANES), C_LANES)
        data_ref[0:3, lanes] = data[0:3]
        data_ref[3:4, lanes] = element.astype(F32)
        data_ref[4:5, lanes] = group.astype(F32)
        data_ref[5:6, lanes] = rank
        return base

    total = lax.fori_loop(0, STEPS, count, jnp.zeros((GROUPS, 1), F32))
    tiles = ((total.astype(I32) + (TILE - 1)) >> 8).astype(F32)
    lower = jnp.where(iota((GROUPS, GROUPS), 1) < iota((GROUPS, GROUPS), 0), 1.0, 0.0)
    start = dot(lower.astype(BF16), jnp.broadcast_to(tiles, (GROUPS, 128)).astype(BF16))[:, 0:1]
    for g in range(GROUPS):
        first_ref[g] = jnp.sum(start[g : g + 1]).astype(I32)
    first_ref[GROUPS] = jnp.sum(tiles).astype(I32)
    used = first_ref[GROUPS]

    def name_group(g, carry):
        def name_tile(t, inner):
            group_ref[t] = g
            return inner

        return lax.fori_loop(first_ref[g], first_ref[g + 1], name_tile, carry)

    lax.fori_loop(0, GROUPS, name_group, 0)
    for n in range(PAIR - 1):
        group_ref[used + n] = 0

    sorted_ref[...] = jnp.zeros_like(sorted_ref)

    def sort(n, first, rows):
        lanes = pl.ds(pl.multiple_of(n * C_LANES, C_LANES), C_LANES)
        group = data_ref[4:5, lanes].astype(I32)
        here = iota((GROUPS, C_LANES), 0) == group
        base = jnp.sum(jnp.where(here, start, 0.0), axis=0, keepdims=True)
        slot = base.astype(I32) * TILE + data_ref[5:6, lanes].astype(I32)
        where_row = onehot(first, rows, jnp.where(group < GROUPS, slot >> 8, -1))
        where_col = onehot(0, TILE, slot & 255)
        at = iota((1, C_LANES), 1)
        late = at - SOURCES * 128
        second = late >= 0
        source = n * SOURCES + jnp.where(second, late >> 6, at >> 7)
        back = flat_slot(source, jnp.where(second, 128 + (late & 63), at & 127))
        lhs = [both(where_row, *parts(data_ref[k : k + 1, lanes])) for k in range(3)]
        lhs.append(both(where_row, ((back >> 8) + 1) * 64, data_ref[3:4, lanes]))
        wide = jnp.concatenate([where_col, where_col], axis=1)
        got = lane_dot(jnp.concatenate(lhs, axis=0), wide)
        last = lane_dot(spread(where_row, back & 255), where_col)
        for k in range(4):
            sorted_ref[k, first : first + rows, :] += got[k * rows : k * rows + rows]
        sorted_ref[4, first : first + rows, :] += last

    def usual(n, carry):
        sort(n, 0, USUAL)
        return carry

    lax.fori_loop(0, STEPS, usual, 0)

    @pl.when(used > USUAL)
    def _():
        def more(n, carry):
            sort(n, USUAL, MOST - USUAL)
            return carry

        lax.fori_loop(0, STEPS, more, 0)

    val_ref[...] = jnp.zeros_like(val_ref)
    load.wait()
    row8 = iota((8, TILE), 0)
    scales = jnp.zeros((8, TILE), F32)
    for i in range(8):
        value = 1.0
        for n in range(8):
            if n != i:
                value = value / (nodes[i] - nodes[n])
        scales = jnp.where(row8 == i, float(value), scales)

    def one_tile(t):
        rows = pl.ds(pl.multiple_of(group_ref[t] * GROUP, GROUP), GROUP)
        table = jnp.concatenate(
            [file_ref[rows, f * 512 : f * 512 + 512] for f in range(FIELDS)], axis=0
        )
        table = jnp.concatenate([table, table], axis=1)
        b0, b1, b2 = [basis_rows(sorted_ref[k, pl.ds(t, 1), :], nodes, scales) for k in range(3)]
        element = sorted_ref[3, pl.ds(t, 1), :].astype(I32) & 63
        planes = jnp.concatenate([b1[j : j + 1] * b2 for j in range(8)], axis=0)
        tops, lows = [], []
        for i in range(8):
            tensor = b0[i : i + 1] * planes
            top = tensor.astype(BF16)
            tops.append(top)
            lows.append((tensor - top.astype(F32)).astype(BF16))
        result = dot(table, jnp.concatenate(tops + lows, axis=0))
        mask = iota((GROUP, TILE), 0) == element
        return [
            jnp.sum(
                jnp.where(mask, result[f * GROUP : f * GROUP + GROUP], 0.0), axis=0, keepdims=True
            )
            for f in range(FIELDS)
        ]

    def on_tiles(n, carry):
        values = [one_tile(n * PAIR + q) for q in range(PAIR)]
        for q in range(PAIR):
            for f in range(FIELDS):
                val_ref[f, pl.ds(n * PAIR + q, 1), :] = values[q][f]
        return carry

    lax.fori_loop(0, (used + PAIR - 1) // PAIR, on_tiles, 0)

    acc_ref[...] = jnp.zeros_like(acc_ref)

    def back(n, carry):
        def row(ref, k):
            lines = [ref[k, pl.ds(n * MANY + q, 1), :] for q in range(MANY)]
            return jnp.concatenate(lines, axis=1)

        where_row = onehot(0, ROWS, (row(sorted_ref, 3).astype(I32) >> 6) - 1)
        where_col = onehot(0, 256, row(sorted_ref, 4))
        wide = jnp.concatenate([where_col, where_col], axis=1)
        lhs = [both(where_row, *parts(row(val_ref, f))) for f in range(FIELDS)]
        acc_ref[...] += lane_dot(jnp.concatenate(lhs, axis=0), wide)
        return carry

    lax.fori_loop(0, (used + MANY - 1) // MANY, back, 0)
    middle = []
    for f in range(FIELDS):
        block = acc_ref[f * ROWS : f * ROWS + ROWS, :]
        flat_ref[pl.ds(0, ROWS, 2), :] = block[:, 0:128]
        flat_ref[pl.ds(1, ROWS, 2), :] = block[:, 128:256]
        out_ref[:, f, :] = flat_ref[pl.ds(0, 64, 3), :]
        out_ref[:, 8 + f, :] = flat_ref[pl.ds(2, 64, 3), :]
        middle.append(flat_ref[pl.ds(1, 64, 3), :])
    middle.append(jnp.zeros_like(middle[0]))
    low = iota((64, 128), 1) < HALF
    for k in range(3):
        left, right = middle[2 * k], middle[2 * k + 1]
        out_ref[:, 5 + k, :] = jnp.where(low, left, pltpu.roll(right, HALF, 1))
        out_ref[:, 13 + k, :] = jnp.where(low, pltpu.roll(left, HALF, 1), right)


def evaluate(recv, span, file_fields):
    return pl.pallas_call(
        evaluate_kernel,
        out_shape=jax.ShapeDtypeStruct((DEVICES // 2, 16, 128), F32),
        in_specs=[
            pl.BlockSpec(memory_space=pltpu.VMEM),
            pl.BlockSpec(memory_space=pltpu.VMEM),
            pl.BlockSpec(memory_space=pl.ANY),
        ],
        out_specs=pl.BlockSpec(memory_space=pltpu.VMEM),
        scratch_shapes=[
            pltpu.VMEM((DEVICES * SPAN, WIDTH), BF16),
            pltpu.VMEM((8, SLOTS), F32),
            pltpu.VMEM((5, MOST, TILE), F32),
            pltpu.VMEM((FIELDS, MOST, TILE), F32),
            pltpu.VMEM((FIELDS * ROWS, 256), F32),
            pltpu.VMEM((2 * ROWS, 128), F32),
            pltpu.SMEM((GROUPS + 1,), I32),
            pltpu.SMEM((MOST + PAIR,), I32),
            pltpu.SemaphoreType.DMA(()),
        ],
        compiler_params=pltpu.CompilerParams(vmem_limit_bytes=56 * 1024 * 1024),
        cost_estimate=pl.CostEstimate(
            flops=60_000_000_000, bytes_accessed=6_000_000, transcendentals=0
        ),
        name="evaluate",
    )(recv, span, file_fields)


E_LANES = 2048
PIECES = 4


def collect_kernel(
    back_ref, slot_ref, moved_hbm, out_ref, owned_hbm, table_ref, flat_ref, held_ref, sems
):
    rows = DEVICES * SPAN // PIECES
    pieces = [pl.ds(n * rows, rows) for n in range(PIECES)]
    loads = [
        pltpu.make_async_copy(moved_hbm.at[p], held_ref.at[p], sems.at[n])
        for n, p in enumerate(pieces)
    ]
    stores = [
        pltpu.make_async_copy(held_ref.at[p], owned_hbm.at[p], sems.at[PIECES + n])
        for n, p in enumerate(pieces)
    ]
    for copy in loads:
        copy.start()
    low = iota((64, 128), 1) < HALF
    for f in range(FIELDS):
        flat_ref[pl.ds(0, 64, 3), :] = back_ref[:, f, :]
        flat_ref[pl.ds(2, 64, 3), :] = back_ref[:, 8 + f, :]
        left, right = back_ref[:, 5 + f // 2, :], back_ref[:, 13 + f // 2, :]
        if f % 2:
            left = pltpu.roll(left, HALF, 1)
        else:
            right = pltpu.roll(right, HALF, 1)
        flat_ref[pl.ds(1, 64, 3), :] = jnp.where(low, left, right)
        for half in range(2):
            high, rest = parts(flat_ref[pl.ds(half, ROWS, 2), :])
            here = slice(f * ROWS, f * ROWS + ROWS)
            table_ref[here, 128 * half : 128 * half + 128] = high.astype(BF16)
            table_ref[here, 256 + 128 * half : 384 + 128 * half] = rest.astype(BF16)

    def step(n, carry):
        lanes = pl.ds(pl.multiple_of(n * E_LANES, E_LANES), E_LANES)
        slot = slot_ref[:, lanes]
        mask = iota((ROWS, E_LANES), 0) == (slot >> 8)
        where_col = onehot(0, 256, slot & 255)
        got = dot(table_ref[...], jnp.concatenate([where_col, where_col], axis=0))
        for f in range(FIELDS):
            out_ref[f : f + 1, lanes] = jnp.sum(
                jnp.where(mask, got[f * ROWS : f * ROWS + ROWS], 0.0), axis=0, keepdims=True
            )
        return carry

    steps = POINTS // E_LANES
    lax.fori_loop(0, steps // 2, step, 0)
    for load, store in zip(loads, stores):
        load.wait()
        store.start()
    lax.fori_loop(steps // 2, steps, step, 0)
    for store in stores:
        store.wait()


def collect(back, slot, moved):
    return pl.pallas_call(
        collect_kernel,
        out_shape=(
            jax.ShapeDtypeStruct((FIELDS, POINTS), F32),
            jax.ShapeDtypeStruct(moved.shape, moved.dtype),
        ),
        in_specs=[
            pl.BlockSpec(memory_space=pltpu.VMEM),
            pl.BlockSpec(memory_space=pltpu.VMEM),
            pl.BlockSpec(memory_space=pl.ANY),
        ],
        out_specs=(pl.BlockSpec(memory_space=pltpu.VMEM), pl.BlockSpec(memory_space=pl.ANY)),
        scratch_shapes=[
            pltpu.VMEM((FIELDS * ROWS, 512), BF16),
            pltpu.VMEM((2 * ROWS, 128), F32),
            pltpu.VMEM((DEVICES * SPAN, WIDTH), BF16),
            pltpu.SemaphoreType.DMA((2 * PIECES,)),
        ],
        compiler_params=pltpu.CompilerParams(vmem_limit_bytes=56 * 1024 * 1024),
        name="collect",
    )(back, slot, moved)


def exchange(x):
    return lax.all_to_all(x, AXES, split_axis=0, concat_axis=0, tiled=True)


def shards(file_fields, span_map, point_dest, point_local, point_coords):
    columns = jnp.arange(DEVICES, dtype=I32)
    inverse = jnp.zeros((DEVICES,), I32).at[span_map[0]].set(columns)
    pieces = file_fields.reshape(DEVICES, SPAN, WIDTH)[inverse]
    sent, slot = bucket(
        point_dest.reshape(1, POINTS), point_local.reshape(1, POINTS), point_coords
    )
    recv = exchange(sent.reshape(DEVICES, 8, 128))
    pieces, recv = lax.optimization_barrier((pieces, recv))
    moved = exchange(pieces).reshape(DEVICES * SPAN, WIDTH)
    values = evaluate(recv, span_map, file_fields)
    values, moved = lax.optimization_barrier((values, moved))
    back = exchange(values.reshape(DEVICES, 8, 128)).reshape(DEVICES // 2, 16, 128)
    return collect(back, slot, moved)


def solution(mesh):
    return jax.shard_map(
        shards,
        mesh=mesh,
        in_specs=(
            P(AXES, None),
            P(AXES, None),
            P(AXES, None),
            P(AXES),
            P(None, AXES),
        ),
        out_specs=(P(None, AXES), P(AXES, None)),
        check_vma=False,
    )
```

time: 219 us -> 140 us (0.64)
  Pallas kernels: 115 us -> 80.4 us
  waiting for transfers between devices: 46.8 us -> 14.6 us
  local copies, waits for them, and re-layouts: 15.3 us -> 6.71 us
  blocking collectives: 22.9 us -> 19.3 us
    pallas_call x3, Pallas kernels: 115 us -> 80.4 us  [the longest x1 55.6 us: evaluate(): pl.pallas_call(evaluate_kernel, out_shape=jax.ShapeDtypeStruct((DEVICES /...]
    all_to_all x2, waiting for transfers between devices: 46.8 us -> 14.6 us  [exchange(): return lax.all_to_all(x, AXES, split_axis=0, concat_axis=0, tiled=True)]
    unnamed x11 -> x2, local copies, waits for them, and re-layouts: 8.6 us -> 0.01 us
    all_to_all x1, blocking collectives: 22.9 us -> 19.3 us  [exchange(): return lax.all_to_all(x, AXES, split_axis=0, concat_axis=0, tiled=True)]
  transfers between devices with their start and end apart: 2 -> 2, of which waited for: 2 -> 2; matrix products, arithmetic and copies ran while one was open for 3% -> 5% of each run, Pallas kernels for 11% -> 40%
where the time goes in v2:
time: 140 us; the launch traced here: 139 us
  Pallas kernels  80.4 us (57%)
  blocking collectives  19.3 us (14%)
  starting transfers between devices  16.8 us (12%)
  waiting for transfers between devices  14.6 us (10%)
  local copies, waits for them, and re-layouts  6.71 us (5%)
    pallas_call x1, Pallas kernels, evaluate(): pl.pallas_call(evaluate_kernel, out_shape=jax.ShapeDtypeStruct((DEVICES /...  55.6 us
    all_to_all x1, blocking collectives, exchange(): return lax.all_to_all(x, AXES, split_axis=0, concat_axis=0, tiled=True)  19.3 us
    all_to_all x2, starting transfers between devices, exchange(): return lax.all_to_all(x, AXES, split_axis=0, concat_axis=0, tiled=True)  16.8 us
    all_to_all x2, waiting for transfers between devices, exchange(): return lax.all_to_all(x, AXES, split_axis=0, concat_axis=0, tiled=True)  14.6 us
    pallas_call x1, Pallas kernels, bucket(): pl.pallas_call(bucket_kernel, out_shape=(jax.ShapeDtypeStruct((DEVICES //...  12.4 us
    pallas_call x1, Pallas kernels, collect(): pl.pallas_call(collect_kernel, out_shape=(jax.ShapeDtypeStruct((FIELDS, P...  12.4 us
    gather x1, local copies, waits for them, and re-layouts, shards(): pieces = file_fields.reshape(DEVICES, SPAN, WIDTH)[inverse]  5.73 us
  transfers between devices with their start and end apart: 2, of which 2 were waited for; matrix products, arithmetic and copies ran while one was open for 5% of the time, Pallas kernels for 40%

profile of v2, /device:TPU:1, one launch (start us, length us, event | category | flops | bytes accessed | tf_op | source)
XLA Modules:
  0.0 139.2 jit_solution(4706401985395435500)
XLA Ops:
  0.6 12.4 %bucket.1 = (f32[64,16,128]{2,1,0:T(8,128)}, s32[1,16384]{1,0:T(1,128)}) custom-call(s32[1,16384]{1,0:T(1,128)} %bitcast.16, s32[1,16384]{1,0:T(1,128)} %bitcast.17, f32[3,16384]{1,0:T(4,128)} %coords_hbm.1), custom_call_target="tpu_custom_call" | custom-call | tf_op jit(solution)/shard_map/bucket/pallas_call | solution.py:169
  13.1 11.4 %all-to-all-start = ((f32[128,8,128]{2,1,0:T(8,128)}), f32[128,8,128]{2,1,0:T(8,128)S(1)}, u32[]{:S(2)}, u32[]{:S(2)}) async-start(f32[128,8,128]{2,1,0:T(8,128)} %bitcast.14), calls=%async_computation | async-start | bytes 1048576 | tf_op jit(solution)/shard_map/all_to_all | solution.py:484
  24.5 0.7 fusion
  25.2 1.0 scatter_custom_fusion
  26.2 5.7 %gather_fusion = bf16[128,8,2560]{2,1,0:T(8,128)(2,1)} fusion(bf16[128,8,2560]{2,1,0:T(8,128)(2,1)} %bitcast.12, s32[1024]{0:T(1024)S(1)} %pad_clamp_fusion), kind=kCustom, calls=%fused_computation | custom fusion | bytes 10486272 | tf_op jit(solution)/shard_map/gather | solution.py:490
  31.9 6.3 %all-to-all-done.recv_ref = f32[128,8,128]{2,1,0:T(8,128)S(1)} async-done(((f32[128,8,128]{2,1,0:T(8,128)}), f32[128,8,128]{2,1,0:T(8,128)S(1)}, u32[]{:S(2)}, u32[]{:S(2)}) %all-to-all-start) | async-done | bytes 524320 | tf_op jit(solution)/shard_map/all_to_all | solution.py:484
  38.2 0.0 copy-start
  38.2 5.4 %all-to-all-start.1 = ((bf16[128,8,2560]{2,1,0:T(8,128)(2,1)}), bf16[128,8,2560]{2,1,0:T(8,128)(2,1)}, u32[]{:S(2)}, u32[]{:S(2)}) async-start(bf16[128,8,2560]{2,1,0:T(8,128)(2,1)} %gather_fusion), calls=%async_computation.1 | async-start | bytes 10485760 | tf_op jit(solution)/shard_map/all_to_all | solution.py:484
  43.6 0.0 copy-done
  43.6 55.6 %evaluate.1 = f32[64,16,128]{2,1,0:T(8,128)} custom-call(f32[128,8,128]{2,1,0:T(8,128)} %copy-done, s32[1,128]{1,0:T(1,128)} %span_ref.1, bf16[1024,2560]{1,0:T(8,128)(2,1)} %file_hbm.1), custom_call_target="tpu_custom_call" | custom-call | flops 60000002048 | bytes 6000000 | tf_op jit(solution)/shard_map/evaluate/pallas_call | solution.py:374
  99.2 8.3 %all-to-all-done.1 = bf16[128,8,2560]{2,1,0:T(8,128)(2,1)} async-done(((bf16[128,8,2560]{2,1,0:T(8,128)(2,1)}), bf16[128,8,2560]{2,1,0:T(8,128)(2,1)}, u32[]{:S(2)}, u32[]{:S(2)}) %all-to-all-start.1) | async-done | bytes 5242912 | tf_op jit(solution)/shard_map/all_to_all | solution.py:484
  107.5 19.3 %all_to_all.15 = f32[128,8,128]{2,1,0:T(8,128)} all-to-all(f32[128,8,128]{2,1,0:T(8,128)} %bitcast.15), channel_id=1, replica_groups=mesh['owner'=64,'sub'=2] {'owner','sub'}, dimensions={0} | all-to-all | bytes 1048576 | tf_op jit(solution)/shard_map/all_to_all | solution.py:484
  126.8 12.4 %collect.1 = (f32[5,16384]{1,0:T(8,128)}, bf16[1024,2560]{1,0:T(8,128)(2,1)}) custom-call(f32[64,16,128]{2,1,0:T(8,128)} %bitcast.13, s32[1,16384]{1,0:T(1,128)} %get-tuple-element.12.slot_ref, bf16[1024,2560]{1,0:T(8,128)(2,1)} %bitcast.6.moved_hbm), custom_call_target="tpu_custom_call" | custom-call | tf_op jit(solution)/shard_map/collect/pallas_call | solution.py:460
  (3 shorter events, 0.0 us)
Async XLA Ops:
  13.1 25.2 %all-to-all-start = ((f32[128,8,128]{2,1,0:T(8,128)}), f32[128,8,128]{2,1,0:T(8,128)S(1)}, u32[]{:S(2)}, u32[]{:S(2)}) async-start(f32[128,8,128]{2,1,0:T(8,128)} %bitcast.14), calls=%async_computation | async-start | bytes 1048576 | tf_op jit(solution)/shard_map/all_to_all | solution.py:484
  38.2 5.4 %copy-start = (f32[128,8,128]{2,1,0:T(8,128)}, f32[128,8,128]{2,1,0:T(8,128)S(1)}, u32[]{:S(2)}) copy-start(f32[128,8,128]{2,1,0:T(8,128)S(1)} %all-to-all-done.recv_ref) | copy-start | bytes 1572868
  38.2 69.3 %all-to-all-start.1 = ((bf16[128,8,2560]{2,1,0:T(8,128)(2,1)}), bf16[128,8,2560]{2,1,0:T(8,128)(2,1)}, u32[]{:S(2)}, u32[]{:S(2)}) async-start(bf16[128,8,2560]{2,1,0:T(8,128)(2,1)} %gather_fusion), calls=%async_computation.1 | async-start | bytes 10485760 | tf_op jit(solution)/shard_map/all_to_all | solution.py:484

commit v3 on v2

--- a/solution.py
+++ b/solution.py
@@ -105,7 +105,31 @@
     return block * CAP + jnp.where(odd, jnp.where(late, place - 128, place + 64), place)
 
 
-A_LANES = 2048
+def to_grid(x):
+    return ((x + 1.0) * 32767.5 + 0.5).astype(I32).astype(F32)
+
+
+def from_grid(x):
+    return x * (1.0 / 32767.5) - 1.0
+
+
+def low_half(word):
+    return (word << 16) >> 16
+
+
+def high_half(word):
+    return word >> 16
+
+
+def left_halves(a, b):
+    return jnp.where(iota(a.shape, 1) < HALF, a, pltpu.roll(b, HALF, 1))
+
+
+def right_halves(a, b):
+    return jnp.where(iota(a.shape, 1) < HALF, pltpu.roll(a, HALF, 1), b)
+
+
+A_LANES = 4096
 
 
 def bucket_kernel(
@@ -136,7 +160,7 @@
         slot = slot_ref[:, at(n)]
         where_row = onehot(0, ROWS, slot >> 8)
         where_col = onehot(0, 256, slot & 255)
-        rows = [both(where_row, *parts(coords_ref[k : k + 1, at(n)])) for k in range(3)]
+        rows = [both(where_row, *parts(to_grid(coords_ref[k : k + 1, at(n)]))) for k in range(3)]
         rows.append(both(where_row, dest_ref[:, at(n)] * 8 + 8, local_ref[:, at(n)] & 7))
         wide = jnp.concatenate([where_col, where_col], axis=1)
         return lane_dot(jnp.concatenate(rows, axis=0), wide)
@@ -154,22 +178,28 @@
 
     lax.fori_loop(0, steps - 1, step, base)
     acc_ref[...] += scatter(steps - 1)
-    for k in range(4):
-        block = acc_ref[k * ROWS : k * ROWS + ROWS, :]
+    middle = []
+    for k in range(2):
+        low, high = [
+            acc_ref[q * ROWS : q * ROWS + ROWS, :].astype(I32) for q in (2 * k, 2 * k + 1)
+        ]
+        block = low + (high << 16)
         flat_ref[pl.ds(0, ROWS, 2), :] = block[:, 0:128]
         flat_ref[pl.ds(1, ROWS, 2), :] = block[:, 128:256]
         out_ref[:, k, :] = flat_ref[pl.ds(0, 64, 3), :]
-        out_ref[:, 8 + k, :] = flat_ref[pl.ds(2, 64, 3), :]
-        middle = flat_ref[pl.ds(1, 64, 3), :]
-        out_ref[:, 4 + k, :] = middle
-        out_ref[:, 12 + k, :] = pltpu.roll(middle, HALF, 1)
+        out_ref[:, 4 + k, :] = flat_ref[pl.ds(2, 64, 3), :]
+        middle.append(flat_ref[pl.ds(1, 64, 3), :])
+    out_ref[:, 2, :] = left_halves(*middle)
+    out_ref[:, 6, :] = right_halves(*middle)
+    out_ref[:, 3, :] = jnp.zeros((64, 128), I32)
+    out_ref[:, 7, :] = jnp.zeros((64, 128), I32)
 
 
 def bucket(dest, local, coords):
     return pl.pallas_call(
         bucket_kernel,
         out_shape=(
-            jax.ShapeDtypeStruct((DEVICES // 2, 16, 128), F32),
+            jax.ShapeDtypeStruct((DEVICES // 2, 8, 128), I32),
             jax.ShapeDtypeStruct((1, POINTS), I32),
         ),
         in_specs=[pl.BlockSpec(memory_space=pl.ANY)] * 3,
@@ -179,7 +209,7 @@
             pltpu.VMEM((1, POINTS), I32),
             pltpu.VMEM((3, POINTS), F32),
             pltpu.VMEM((4 * ROWS, 256), F32),
-            pltpu.VMEM((2 * ROWS, 128), F32),
+            pltpu.VMEM((2 * ROWS, 128), I32),
             pltpu.SemaphoreType.DMA((3,)),
         ],
         compiler_params=pltpu.CompilerParams(vmem_limit_bytes=56 * 1024 * 1024),
@@ -191,6 +221,7 @@
 C_LANES = SOURCES * CAP
 STEPS = DEVICES // SOURCES
 USUAL = 96
+LEVELS = 32600.0
 PAIR = 2
 MANY = 8
 
@@ -213,25 +244,30 @@
     before = earlier(256, 256)
     permutation = jnp.where(iota((128, 128), 0) == span_ref[...], 1.0, 0.0).astype(BF16)
     inverse = lane_dot(iota((16, 128), 1).astype(F32).astype(BF16), permutation).astype(BF16)
-    lane = iota((8, 128), 1)
 
     def count(n, base):
-        source = n * SOURCES
-        blocks = [recv_ref[source + s] for s in range(SOURCES)]
-        pairs = [
-            jnp.where(lane < HALF, blocks[2 * s], pltpu.roll(blocks[2 * s + 1], HALF, 1))
-            for s in range(SOURCES // 2)
+        blocks = [recv_ref[n * (SOURCES // 2) + s] for s in range(SOURCES // 2)]
+        turned = [pltpu.roll(block, HALF, 1) for block in blocks]
+        whole = jnp.concatenate(blocks, axis=1)
+        swapped = jnp.concatenate(turned, axis=1)
+        early = (iota((1, SOURCES * 64), 1) & 127) < HALF
+        words = [
+            jnp.concatenate(
+                [whole[0:1], whole[4:5], jnp.where(early, whole[2:3], swapped[6:7])], axis=1
+            ),
+            jnp.concatenate(
+                [whole[1:2], whole[5:6], jnp.where(early, swapped[2:3], whole[6:7])], axis=1
+            ),
         ]
-        full = jnp.concatenate(blocks, axis=1)[0:4]
-        rest = jnp.concatenate(pairs, axis=1)[4:8]
-        data = jnp.concatenate([full, rest], axis=1)
-        number = data[3:4].astype(I32)
+        number = high_half(words[1])
         span = dot(inverse, onehot(0, 128, (number >> 3) - 1))[0:1].astype(I32)
         group = jnp.where(number > 0, span >> 3, GROUPS)
         element = (span & 7) * 8 + (number & 7)
         rank, base = ranks(iota((GROUPS, C_LANES), 0) == group, before, base)
         lanes = pl.ds(pl.multiple_of(n * C_LANES, C_LANES), C_LANES)
-        data_ref[0:3, lanes] = data[0:3]
+        data_ref[0:1, lanes] = (words[0] & 0xFFFF).astype(F32)
+        data_ref[1:2, lanes] = (high_half(words[0]) & 0xFFFF).astype(F32)
+        data_ref[2:3, lanes] = (words[1] & 0xFFFF).astype(F32)
         data_ref[3:4, lanes] = element.astype(F32)
         data_ref[4:5, lanes] = group.astype(F32)
         data_ref[5:6, lanes] = rank
@@ -268,10 +304,10 @@
         where_row = onehot(first, rows, jnp.where(group < GROUPS, slot >> 8, -1))
         where_col = onehot(0, TILE, slot & 255)
         at = iota((1, C_LANES), 1)
-        late = at - SOURCES * 128
-        second = late >= 0
-        source = n * SOURCES + jnp.where(second, late >> 6, at >> 7)
-        back = flat_slot(source, jnp.where(second, 128 + (late & 63), at & 127))
+        pair = n * (SOURCES // 2) + ((at >> 7) & (SOURCES // 2 - 1))
+        third = at >= SOURCES * 128
+        odd = jnp.where(third, (at >> 6) & 1, jnp.where(at >= SOURCES * 64, 1, 0))
+        back = flat_slot(2 * pair + odd, jnp.where(third, 128 + (at & 63), at & 127))
         lhs = [both(where_row, *parts(data_ref[k : k + 1, lanes])) for k in range(3)]
         lhs.append(both(where_row, ((back >> 8) + 1) * 64, data_ref[3:4, lanes]))
         wide = jnp.concatenate([where_col, where_col], axis=1)
@@ -312,7 +348,7 @@
             [file_ref[rows, f * 512 : f * 512 + 512] for f in range(FIELDS)], axis=0
         )
         table = jnp.concatenate([table, table], axis=1)
-        b0, b1, b2 = [basis_rows(sorted_ref[k, pl.ds(t, 1), :], nodes, scales) for k in range(3)]
+        b0, b1, b2 = [basis_rows(from_grid(sorted_ref[k, pl.ds(t, 1), :]), nodes, scales) for k in range(3)]
         element = sorted_ref[3, pl.ds(t, 1), :].astype(I32) & 63
         planes = jnp.concatenate([b1[j : j + 1] * b2 for j in range(8)], axis=0)
         tops, lows = [], []
@@ -354,26 +390,49 @@
         return carry
 
     lax.fori_loop(0, (used + MANY - 1) // MANY, back, 0)
-    middle = []
+    evens, odds, middle = [], [], []
     for f in range(FIELDS):
         block = acc_ref[f * ROWS : f * ROWS + ROWS, :]
         flat_ref[pl.ds(0, ROWS, 2), :] = block[:, 0:128]
         flat_ref[pl.ds(1, ROWS, 2), :] = block[:, 128:256]
-        out_ref[:, f, :] = flat_ref[pl.ds(0, 64, 3), :]
-        out_ref[:, 8 + f, :] = flat_ref[pl.ds(2, 64, 3), :]
+        evens.append(flat_ref[pl.ds(0, 64, 3), :])
+        odds.append(flat_ref[pl.ds(2, 64, 3), :])
         middle.append(flat_ref[pl.ds(1, 64, 3), :])
-    middle.append(jnp.zeros_like(middle[0]))
     low = iota((64, 128), 1) < HALF
-    for k in range(3):
-        left, right = middle[2 * k], middle[2 * k + 1]
-        out_ref[:, 5 + k, :] = jnp.where(low, left, pltpu.roll(right, HALF, 1))
-        out_ref[:, 13 + k, :] = jnp.where(low, pltpu.roll(left, HALF, 1), right)
+
+    def exponent(firsts, own):
+        most = jnp.zeros((64, 128), F32)
+        for first, mid in zip(firsts, middle):
+            most = jnp.maximum(most, jnp.abs(first))
+            most = jnp.maximum(most, jnp.where(own, jnp.abs(mid), 0.0))
+        most = jnp.max(most, axis=1, keepdims=True)
+        power = jnp.ceil(jnp.log2(jnp.maximum(most, 1e-30)))
+        return jnp.broadcast_to(power, (64, 128))
+
+    def coded(value, factor):
+        return jnp.floor(value * factor + 0.5).astype(I32)
+
+    def word(a, b):
+        return (a & 0xFFFF) | (b << 16)
+
+    powers = [exponent(evens, low), exponent(odds, jnp.logical_not(low))]
+    factors = [LEVELS * jnp.exp2(-power) for power in powers]
+    last = [coded(mid, jnp.where(low, factors[0], factors[1])) for mid in middle]
+    for odd, firsts in enumerate((evens, odds)):
+        halves = right_halves if odd else left_halves
+        first = [coded(value, factors[odd]) for value in firsts]
+        power = powers[odd].astype(I32)
+        out_ref[:, 4 * odd, :] = word(first[0], first[1])
+        out_ref[:, 4 * odd + 1, :] = word(first[2], first[3])
+        out_ref[:, 4 * odd + 2, :] = word(first[4], halves(last[0], last[1]))
+        tail = pltpu.roll(last[3], HALF, 1) if odd else last[3]
+        out_ref[:, 4 * odd + 3, :] = word(halves(last[2], last[4]), jnp.where(low, tail, power))
 
 
 def evaluate(recv, span, file_fields):
     return pl.pallas_call(
         evaluate_kernel,
-        out_shape=jax.ShapeDtypeStruct((DEVICES // 2, 16, 128), F32),
+        out_shape=jax.ShapeDtypeStruct((DEVICES // 2, 8, 128), I32),
         in_specs=[
             pl.BlockSpec(memory_space=pltpu.VMEM),
             pl.BlockSpec(memory_space=pltpu.VMEM),
@@ -418,16 +477,30 @@
     ]
     for copy in loads:
         copy.start()
-    low = iota((64, 128), 1) < HALF
+    firsts, lasts = [], []
+    for odd in range(2):
+        words = [back_ref[:, 4 * odd + r, :] for r in range(4)]
+        tail = high_half(words[3])
+        factor = jnp.exp2(right_halves(tail, tail).astype(F32)) * (1.0 / LEVELS)
+        firsts.append(
+            [
+                half(words[r]).astype(F32) * factor
+                for r, half in (
+                    (0, low_half), (0, high_half), (1, low_half), (1, high_half), (2, low_half)
+                )
+            ]
+        )
+        lasts.append(
+            [
+                value.astype(F32) * factor
+                for value in (high_half(words[2]), low_half(words[3]), tail)
+            ]
+        )
     for f in range(FIELDS):
-        flat_ref[pl.ds(0, 64, 3), :] = back_ref[:, f, :]
-        flat_ref[pl.ds(2, 64, 3), :] = back_ref[:, 8 + f, :]
-        left, right = back_ref[:, 5 + f // 2, :], back_ref[:, 13 + f // 2, :]
-        if f % 2:
-            left = pltpu.roll(left, HALF, 1)
-        else:
-            right = pltpu.roll(right, HALF, 1)
-        flat_ref[pl.ds(1, 64, 3), :] = jnp.where(low, left, right)
+        flat_ref[pl.ds(0, 64, 3), :] = firsts[0][f]
+        flat_ref[pl.ds(2, 64, 3), :] = firsts[1][f]
+        k, halves = ((0, left_halves), (0, right_halves), (1, left_halves), (2, left_halves), (1, right_halves))[f]
+        flat_ref[pl.ds(1, 64, 3), :] = halves(lasts[0][k], lasts[1][k])
         for half in range(2):
             high, rest = parts(flat_ref[pl.ds(half, ROWS, 2), :])
             here = slice(f * ROWS, f * ROWS + ROWS)
@@ -447,11 +520,11 @@
         return carry
 
     steps = POINTS // E_LANES
-    lax.fori_loop(0, steps // 2, step, 0)
+    lax.fori_loop(0, steps // 2, step, 0, unroll=True)
     for load, store in zip(loads, stores):
         load.wait()
         store.start()
-    lax.fori_loop(steps // 2, steps, step, 0)
+    lax.fori_loop(steps // 2, steps, step, 0, unroll=True)
     for store in stores:
         store.wait()
 
@@ -491,12 +564,12 @@
     sent, slot = bucket(
         point_dest.reshape(1, POINTS), point_local.reshape(1, POINTS), point_coords
     )
-    recv = exchange(sent.reshape(DEVICES, 8, 128))
+    recv = exchange(sent.reshape(DEVICES, 4, 128)).reshape(DEVICES // 2, 8, 128)
     pieces, recv = lax.optimization_barrier((pieces, recv))
     moved = exchange(pieces).reshape(DEVICES * SPAN, WIDTH)
     values = evaluate(recv, span_map, file_fields)
     values, moved = lax.optimization_barrier((values, moved))
-    back = exchange(values.reshape(DEVICES, 8, 128)).reshape(DEVICES // 2, 16, 128)
+    back = exchange(values.reshape(DEVICES, 4, 128)).reshape(DEVICES // 2, 8, 128)
     return collect(back, slot, moved)
 
 

time: 140 us -> 134 us (0.957)
  waiting for transfers between devices: 14.6 us -> 11.8 us
  blocking collectives: 19.3 us -> 16.6 us
  Pallas kernels: 80.4 us -> 78.5 us
    all_to_all x2, waiting for transfers between devices: 14.6 us -> 11.8 us  [exchange(): return lax.all_to_all(x, AXES, split_axis=0, concat_axis=0, tiled=True)]
    all_to_all x1, blocking collectives: 19.3 us -> 16.6 us  [exchange(): return lax.all_to_all(x, AXES, split_axis=0, concat_axis=0, tiled=True)]
  transfers between devices with their start and end apart: 2 -> 2, of which waited for: 2 -> 2; matrix products, arithmetic and copies ran while one was open for 5% -> 6% of each run, Pallas kernels for 40% -> 42%
where the time goes in v3:
time: 134 us
  Pallas kernels  78.5 us (59%)
  starting transfers between devices  18 us (13%)
  blocking collectives  16.6 us (12%)
  waiting for transfers between devices  11.8 us (9%)
  local copies, waits for them, and re-layouts  7.41 us (6%)
    pallas_call x1, Pallas kernels, evaluate(): pl.pallas_call(evaluate_kernel, out_shape=jax.ShapeDtypeStruct((DEVICES /...  55.7 us
    all_to_all x2, starting transfers between devices, exchange(): return lax.all_to_all(x, AXES, split_axis=0, concat_axis=0, tiled=True)  18 us
    all_to_all x1, blocking collectives, exchange(): return lax.all_to_all(x, AXES, split_axis=0, concat_axis=0, tiled=True)  16.6 us
    all_to_all x2, waiting for transfers between devices, exchange(): return lax.all_to_all(x, AXES, split_axis=0, concat_axis=0, tiled=True)  11.8 us
    pallas_call x1, Pallas kernels, collect(): pl.pallas_call(collect_kernel, out_shape=(jax.ShapeDtypeStruct((FIELDS, P...  11.4 us
    pallas_call x1, Pallas kernels, bucket(): pl.pallas_call(bucket_kernel, out_shape=(jax.ShapeDtypeStruct((DEVICES //...  11.4 us
    gather x1, local copies, waits for them, and re-layouts, shards(): pieces = file_fields.reshape(DEVICES, SPAN, WIDTH)[inverse]  5.73 us
  transfers between devices with their start and end apart: 2, of which 2 were waited for; matrix products, arithmetic and copies ran while one was open for 6% of the time, Pallas kernels for 42%

profile of v3, /device:TPU:1, one launch (start us, length us, event | category | flops | bytes accessed | tf_op | source)
XLA Modules:
  0.0 133.8 jit_solution(12674018872205400663)
XLA Ops:
  0.6 11.4 %bucket.1 = (s32[64,8,128]{2,1,0:T(8,128)}, s32[1,16384]{1,0:T(1,128)}) custom-call(s32[1,16384]{1,0:T(1,128)} %bitcast.18, s32[1,16384]{1,0:T(1,128)} %bitcast.19, f32[3,16384]{1,0:T(4,128)} %coords_hbm.1), custom_call_target="tpu_custom_call" | custom-call | tf_op jit(solution)/shard_map/bucket/pallas_call | solution.py:199
  12.0 11.5 %all-to-all-start = ((s32[128,4,128]{2,1,0:T(4,128)}), s32[128,4,128]{2,1,0:T(4,128)S(1)}, u32[]{:S(2)}, u32[]{:S(2)}) async-start(s32[128,4,128]{2,1,0:T(4,128)} %bitcast.16), calls=%async_computation | async-start | bytes 524288 | tf_op jit(solution)/shard_map/all_to_all | solution.py:557
  23.6 0.7 fusion
  24.2 1.0 scatter_custom_fusion
  25.2 5.7 %gather_fusion = bf16[128,8,2560]{2,1,0:T(8,128)(2,1)} fusion(bf16[128,8,2560]{2,1,0:T(8,128)(2,1)} %bitcast.13, s32[1024]{0:T(1024)S(1)} %pad_clamp_fusion), kind=kCustom, calls=%fused_computation | custom fusion | bytes 10486272 | tf_op jit(solution)/shard_map/gather | solution.py:563
  31.0 3.7 %all-to-all-done = s32[128,4,128]{2,1,0:T(4,128)S(1)} async-done(((s32[128,4,128]{2,1,0:T(4,128)}), s32[128,4,128]{2,1,0:T(4,128)S(1)}, u32[]{:S(2)}, u32[]{:S(2)}) %all-to-all-start) | async-done | bytes 262176 | tf_op jit(solution)/shard_map/all_to_all | solution.py:557
  34.7 0.0 copy-start
  34.7 0.7 copy-done
  35.4 6.5 %all-to-all-start.1 = ((bf16[128,8,2560]{2,1,0:T(8,128)(2,1)}), bf16[128,8,2560]{2,1,0:T(8,128)(2,1)}, u32[]{:S(2)}, u32[]{:S(2)}) async-start(bf16[128,8,2560]{2,1,0:T(8,128)(2,1)} %gather_fusion), calls=%async_computation.1 | async-start | bytes 10485760 | tf_op jit(solution)/shard_map/all_to_all | solution.py:557
  41.8 55.7 %evaluate.1 = s32[64,8,128]{2,1,0:T(8,128)} custom-call(s32[64,8,128]{2,1,0:T(8,128)} %bitcast.15, s32[1,128]{1,0:T(1,128)} %span_ref.1, bf16[1024,2560]{1,0:T(8,128)(2,1)} %file_hbm.1), custom_call_target="tpu_custom_call" | custom-call | flops 60000002048 | bytes 6000000 | tf_op jit(solution)/shard_map/evaluate/pallas_call | solution.py:433
  97.5 8.1 %all-to-all-done.1 = bf16[128,8,2560]{2,1,0:T(8,128)(2,1)} async-done(((bf16[128,8,2560]{2,1,0:T(8,128)(2,1)}), bf16[128,8,2560]{2,1,0:T(8,128)(2,1)}, u32[]{:S(2)}, u32[]{:S(2)}) %all-to-all-start.1) | async-done | bytes 5242912 | tf_op jit(solution)/shard_map/all_to_all | solution.py:557
  105.6 16.6 %all_to_all.15 = s32[128,4,128]{2,1,0:T(4,128)} all-to-all(s32[128,4,128]{2,1,0:T(4,128)} %bitcast.17), channel_id=1, replica_groups=mesh['owner'=64,'sub'=2] {'owner','sub'}, dimensions={0} | all-to-all | bytes 524288 | tf_op jit(solution)/shard_map/all_to_all | solution.py:557
  122.2 11.4 %collect.1 = (f32[5,16384]{1,0:T(8,128)}, bf16[1024,2560]{1,0:T(8,128)(2,1)}) custom-call(s32[64,8,128]{2,1,0:T(8,128)} %bitcast.14, s32[1,16384]{1,0:T(1,128)} %get-tuple-element.12.slot_ref, bf16[1024,2560]{1,0:T(8,128)(2,1)} %bitcast.7.moved_hbm), custom_call_target="tpu_custom_call" | custom-call | tf_op jit(solution)/shard_map/collect/pallas_call | solution.py:533
  (3 shorter events, 0.0 us)
Async XLA Ops:
  12.0 22.6 %all-to-all-start = ((s32[128,4,128]{2,1,0:T(4,128)}), s32[128,4,128]{2,1,0:T(4,128)S(1)}, u32[]{:S(2)}, u32[]{:S(2)}) async-start(s32[128,4,128]{2,1,0:T(4,128)} %bitcast.16), calls=%async_computation | async-start | bytes 524288 | tf_op jit(solution)/shard_map/all_to_all | solution.py:557
  34.7 0.7 copy-start
  35.4 70.2 %all-to-all-start.1 = ((bf16[128,8,2560]{2,1,0:T(8,128)(2,1)}), bf16[128,8,2560]{2,1,0:T(8,128)(2,1)}, u32[]{:S(2)}, u32[]{:S(2)}) async-start(bf16[128,8,2560]{2,1,0:T(8,128)(2,1)} %gather_fusion), calls=%async_computation.1 | async-start | bytes 10485760 | tf_op jit(solution)/shard_map/all_to_all | solution.py:557

commit v4 on v3

--- a/solution.py
+++ b/solution.py
@@ -217,13 +217,13 @@
     )(dest, local, coords)
 
 
-SOURCES = 16
+SOURCES = 32
 C_LANES = SOURCES * CAP
 STEPS = DEVICES // SOURCES
 USUAL = 96
 LEVELS = 32600.0
-PAIR = 2
-MANY = 8
+PAIR = 8
+MANY = 16
 
 
 def basis_rows(x, nodes, scale):

time: 134 us -> 134 us (level)
  Pallas kernels: 78.5 us -> 71.1 us
  waiting for transfers between devices: 11.8 us -> 19.2 us
    pallas_call x1, Pallas kernels: 55.7 us -> 48.3 us  [evaluate(): pl.pallas_call(evaluate_kernel, out_shape=jax.ShapeDtypeStruct((DEVICES /...]
    all_to_all x2, waiting for transfers between devices: 11.8 us -> 19.2 us  [exchange(): return lax.all_to_all(x, AXES, split_axis=0, concat_axis=0, tiled=True)]
  transfers between devices with their start and end apart: 2 -> 2, of which waited for: 2 -> 2; matrix products, arithmetic and copies ran while one was open for 6% -> 6% of each run, Pallas kernels for 42% -> 36%
where the time goes in v4:
time: 134 us
  Pallas kernels  71.1 us (53%)
  waiting for transfers between devices  19.2 us (14%)
  starting transfers between devices  18 us (13%)
  blocking collectives  16.6 us (12%)
  local copies, waits for them, and re-layouts  7.41 us (6%)
    pallas_call x1, Pallas kernels, evaluate(): pl.pallas_call(evaluate_kernel, out_shape=jax.ShapeDtypeStruct((DEVICES /...  48.3 us
    all_to_all x2, waiting for transfers between devices, exchange(): return lax.all_to_all(x, AXES, split_axis=0, concat_axis=0, tiled=True)  19.2 us
    all_to_all x2, starting transfers between devices, exchange(): return lax.all_to_all(x, AXES, split_axis=0, concat_axis=0, tiled=True)  18 us
    all_to_all x1, blocking collectives, exchange(): return lax.all_to_all(x, AXES, split_axis=0, concat_axis=0, tiled=True)  16.6 us
    pallas_call x1, Pallas kernels, collect(): pl.pallas_call(collect_kernel, out_shape=(jax.ShapeDtypeStruct((FIELDS, P...  11.4 us
    pallas_call x1, Pallas kernels, bucket(): pl.pallas_call(bucket_kernel, out_shape=(jax.ShapeDtypeStruct((DEVICES //...  11.4 us
    gather x1, local copies, waits for them, and re-layouts, shards(): pieces = file_fields.reshape(DEVICES, SPAN, WIDTH)[inverse]  5.73 us
  transfers between devices with their start and end apart: 2, of which 2 were waited for; matrix products, arithmetic and copies ran while one was open for 6% of the time, Pallas kernels for 36%

profile of v4, /device:TPU:1, one launch (start us, length us, event | category | flops | bytes accessed | tf_op | source)
XLA Modules:
  0.0 133.8 jit_solution(12702598193042285019)
XLA Ops:
  0.6 11.4 %bucket.1 = (s32[64,8,128]{2,1,0:T(8,128)}, s32[1,16384]{1,0:T(1,128)}) custom-call(s32[1,16384]{1,0:T(1,128)} %bitcast.18, s32[1,16384]{1,0:T(1,128)} %bitcast.19, f32[3,16384]{1,0:T(4,128)} %coords_hbm.1), custom_call_target="tpu_custom_call" | custom-call | tf_op jit(solution)/shard_map/bucket/pallas_call | solution.py:199
  12.0 11.5 %all-to-all-start = ((s32[128,4,128]{2,1,0:T(4,128)}), s32[128,4,128]{2,1,0:T(4,128)S(1)}, u32[]{:S(2)}, u32[]{:S(2)}) async-start(s32[128,4,128]{2,1,0:T(4,128)} %bitcast.16), calls=%async_computation | async-start | bytes 524288 | tf_op jit(solution)/shard_map/all_to_all | solution.py:557
  23.6 0.7 fusion
  24.2 1.0 scatter_custom_fusion
  25.2 5.7 %gather_fusion = bf16[128,8,2560]{2,1,0:T(8,128)(2,1)} fusion(bf16[128,8,2560]{2,1,0:T(8,128)(2,1)} %bitcast.13, s32[1024]{0:T(1024)S(1)} %pad_clamp_fusion), kind=kCustom, calls=%fused_computation | custom fusion | bytes 10486272 | tf_op jit(solution)/shard_map/gather | solution.py:563
  31.0 3.7 %all-to-all-done = s32[128,4,128]{2,1,0:T(4,128)S(1)} async-done(((s32[128,4,128]{2,1,0:T(4,128)}), s32[128,4,128]{2,1,0:T(4,128)S(1)}, u32[]{:S(2)}, u32[]{:S(2)}) %all-to-all-start) | async-done | bytes 262176 | tf_op jit(solution)/shard_map/all_to_all | solution.py:557
  34.7 0.0 copy-start
  34.7 0.7 copy-done
  35.4 6.5 %all-to-all-start.1 = ((bf16[128,8,2560]{2,1,0:T(8,128)(2,1)}), bf16[128,8,2560]{2,1,0:T(8,128)(2,1)}, u32[]{:S(2)}, u32[]{:S(2)}) async-start(bf16[128,8,2560]{2,1,0:T(8,128)(2,1)} %gather_fusion), calls=%async_computation.1 | async-start | bytes 10485760 | tf_op jit(solution)/shard_map/all_to_all | solution.py:557
  41.8 48.3 %evaluate.1 = s32[64,8,128]{2,1,0:T(8,128)} custom-call(s32[64,8,128]{2,1,0:T(8,128)} %bitcast.15, s32[1,128]{1,0:T(1,128)} %span_ref.1, bf16[1024,2560]{1,0:T(8,128)(2,1)} %file_hbm.1), custom_call_target="tpu_custom_call" | custom-call | flops 60000002048 | bytes 6000000 | tf_op jit(solution)/shard_map/evaluate/pallas_call | solution.py:433
  90.1 15.5 %all-to-all-done.1 = bf16[128,8,2560]{2,1,0:T(8,128)(2,1)} async-done(((bf16[128,8,2560]{2,1,0:T(8,128)(2,1)}), bf16[128,8,2560]{2,1,0:T(8,128)(2,1)}, u32[]{:S(2)}, u32[]{:S(2)}) %all-to-all-start.1) | async-done | bytes 5242912 | tf_op jit(solution)/shard_map/all_to_all | solution.py:557
  105.6 16.6 %all_to_all.15 = s32[128,4,128]{2,1,0:T(4,128)} all-to-all(s32[128,4,128]{2,1,0:T(4,128)} %bitcast.17), channel_id=1, replica_groups=mesh['owner'=64,'sub'=2] {'owner','sub'}, dimensions={0} | all-to-all | bytes 524288 | tf_op jit(solution)/shard_map/all_to_all | solution.py:557
  122.2 11.4 %collect.1 = (f32[5,16384]{1,0:T(8,128)}, bf16[1024,2560]{1,0:T(8,128)(2,1)}) custom-call(s32[64,8,128]{2,1,0:T(8,128)} %bitcast.14, s32[1,16384]{1,0:T(1,128)} %get-tuple-element.12.slot_ref, bf16[1024,2560]{1,0:T(8,128)(2,1)} %bitcast.7.moved_hbm), custom_call_target="tpu_custom_call" | custom-call | tf_op jit(solution)/shard_map/collect/pallas_call | solution.py:533
  (3 shorter events, 0.0 us)
Async XLA Ops:
  12.0 22.6 %all-to-all-start = ((s32[128,4,128]{2,1,0:T(4,128)}), s32[128,4,128]{2,1,0:T(4,128)S(1)}, u32[]{:S(2)}, u32[]{:S(2)}) async-start(s32[128,4,128]{2,1,0:T(4,128)} %bitcast.16), calls=%async_computation | async-start | bytes 524288 | tf_op jit(solution)/shard_map/all_to_all | solution.py:557
  34.7 0.7 copy-start
  35.4 70.2 %all-to-all-start.1 = ((bf16[128,8,2560]{2,1,0:T(8,128)(2,1)}), bf16[128,8,2560]{2,1,0:T(8,128)(2,1)}, u32[]{:S(2)}, u32[]{:S(2)}) async-start(bf16[128,8,2560]{2,1,0:T(8,128)(2,1)} %gather_fusion), calls=%async_computation.1 | async-start | bytes 10485760 | tf_op jit(solution)/shard_map/all_to_all | solution.py:557

commit v5 on v4

--- a/solution.py
+++ b/solution.py
@@ -90,9 +90,11 @@
     ones = jnp.where(mask, 1.0, 0.0)
     narrow = ones.astype(BF16)
     counts = []
-    for j in range(mask.shape[1] // 256):
-        part = slice(256 * j, 256 * j + 256)
-        inside = dot(narrow[:, part], before)
+    rows, blocks = mask.shape[0], mask.shape[1] // 256
+    stacked = [narrow[:, 256 * j : 256 * j + 256] for j in range(blocks)]
+    stacked = dot(jnp.concatenate(stacked, axis=0), before)
+    for j in range(blocks):
+        inside = stacked[rows * j : rows * j + rows]
         counts.append(inside + base)
         base = base + inside[:, 255:256] + ones[:, 256 * j + 255 : 256 * j + 256]
     count = jnp.concatenate(counts, axis=1)
@@ -135,10 +137,16 @@
 def bucket_kernel(
     dest_hbm, local_hbm, coords_hbm, out_ref, slot_ref, dest_ref, local_ref, coords_ref, acc_ref, flat_ref, sems
 ):
+    early, late = pl.ds(0, A_LANES), pl.ds(A_LANES, POINTS - A_LANES)
     copies = [
         pltpu.make_async_copy(src, dst, sems.at[n])
         for n, (src, dst) in enumerate(
-            [(local_hbm, local_ref), (dest_hbm, dest_ref), (coords_hbm, coords_ref)]
+            [
+                (local_hbm.at[:, early], local_ref.at[:, early]),
+                (local_hbm.at[:, late], local_ref.at[:, late]),
+                (dest_hbm, dest_ref),
+                (coords_hbm, coords_ref),
+            ]
         )
     ]
     for copy in copies:
@@ -167,8 +175,8 @@
 
     copies[0].wait()
     base = place(0, jnp.zeros((DEVICES, 1), F32))
-    copies[1].wait()
-    copies[2].wait()
+    for copy in copies[1:]:
+        copy.wait()
 
     def step(n, base):
         got = scatter(n)
@@ -210,7 +218,7 @@
             pltpu.VMEM((3, POINTS), F32),
             pltpu.VMEM((4 * ROWS, 256), F32),
             pltpu.VMEM((2 * ROWS, 128), I32),
-            pltpu.SemaphoreType.DMA((3,)),
+            pltpu.SemaphoreType.DMA((4,)),
         ],
         compiler_params=pltpu.CompilerParams(vmem_limit_bytes=56 * 1024 * 1024),
         name="bucket",
@@ -450,7 +458,7 @@
             pltpu.SMEM((MOST + PAIR,), I32),
             pltpu.SemaphoreType.DMA(()),
         ],
-        compiler_params=pltpu.CompilerParams(vmem_limit_bytes=56 * 1024 * 1024),
+        compiler_params=pltpu.CompilerParams(vmem_limit_bytes=50 * 1024 * 1024),
         cost_estimate=pl.CostEstimate(
             flops=60_000_000_000, bytes_accessed=6_000_000, transcendentals=0
         ),

time: 134 us -> 132 us (0.985)
  no operation moved by 1% of the time
where the time goes in v5:
time: 132 us
  Pallas kernels  70 us (53%)
  waiting for transfers between devices  20.1 us (15%)
  starting transfers between devices  18 us (14%)
  blocking collectives  15.7 us (12%)
  local copies, waits for them, and re-layouts  6.71 us (5%)
    pallas_call x1, Pallas kernels, evaluate(): pl.pallas_call(evaluate_kernel, out_shape=jax.ShapeDtypeStruct((DEVICES /...  47.3 us
    all_to_all x2, waiting for transfers between devices, exchange(): return lax.all_to_all(x, AXES, split_axis=0, concat_axis=0, tiled=True)  20.1 us
    all_to_all x2, starting transfers between devices, exchange(): return lax.all_to_all(x, AXES, split_axis=0, concat_axis=0, tiled=True)  18 us
    all_to_all x1, blocking collectives, exchange(): return lax.all_to_all(x, AXES, split_axis=0, concat_axis=0, tiled=True)  15.7 us
    pallas_call x1, Pallas kernels, collect(): pl.pallas_call(collect_kernel, out_shape=(jax.ShapeDtypeStruct((FIELDS, P...  11.4 us
    pallas_call x1, Pallas kernels, bucket(): pl.pallas_call(bucket_kernel, out_shape=(jax.ShapeDtypeStruct((DEVICES //...  11.2 us
    gather x1, local copies, waits for them, and re-layouts, shards(): pieces = file_fields.reshape(DEVICES, SPAN, WIDTH)[inverse]  5.73 us
  transfers between devices with their start and end apart: 2, of which 2 were waited for; matrix products, arithmetic and copies ran while one was open for 6% of the time, Pallas kernels for 36%

profile of v5, /device:TPU:1, one launch (start us, length us, event | category | flops | bytes accessed | tf_op | source)
XLA Modules:
  0.0 132.0 jit_solution(9511725090168381774)
XLA Ops:
  0.6 11.2 %bucket.1 = (s32[64,8,128]{2,1,0:T(8,128)}, s32[1,16384]{1,0:T(1,128)}) custom-call(s32[1,16384]{1,0:T(1,128)} %bitcast.18, s32[1,16384]{1,0:T(1,128)} %bitcast.19, f32[3,16384]{1,0:T(4,128)} %coords_hbm.1), custom_call_target="tpu_custom_call" | custom-call | tf_op jit(solution)/shard_map/bucket/pallas_call | solution.py:207
  11.9 11.5 %all-to-all-start = ((s32[128,4,128]{2,1,0:T(4,128)}), s32[128,4,128]{2,1,0:T(4,128)S(1)}, u32[]{:S(2)}, u32[]{:S(2)}) async-start(s32[128,4,128]{2,1,0:T(4,128)} %bitcast.17), calls=%async_computation | async-start | bytes 524288 | tf_op jit(solution)/shard_map/all_to_all | solution.py:565
  23.3 0.7 fusion
  24.0 1.0 scatter_custom_fusion
  25.0 5.7 %gather_fusion = bf16[128,8,2560]{2,1,0:T(8,128)(2,1)} fusion(bf16[128,8,2560]{2,1,0:T(8,128)(2,1)} %bitcast.15, s32[1024]{0:T(1024)S(1)} %pad_clamp_fusion), kind=kCustom, calls=%fused_computation | custom fusion | bytes 10486272 | tf_op jit(solution)/shard_map/gather | solution.py:571
  30.7 3.7 %all-to-all-done = s32[128,4,128]{2,1,0:T(4,128)S(1)} async-done(((s32[128,4,128]{2,1,0:T(4,128)}), s32[128,4,128]{2,1,0:T(4,128)S(1)}, u32[]{:S(2)}, u32[]{:S(2)}) %all-to-all-start) | async-done | bytes 262176 | tf_op jit(solution)/shard_map/all_to_all | solution.py:565
  34.4 0.0 copy-start
  34.4 6.5 %all-to-all-start.1 = ((bf16[128,8,2560]{2,1,0:T(8,128)(2,1)}), bf16[128,8,2560]{2,1,0:T(8,128)(2,1)}, u32[]{:S(2)}, u32[]{:S(2)}) async-start(bf16[128,8,2560]{2,1,0:T(8,128)(2,1)} %gather_fusion), calls=%async_computation.1 | async-start | bytes 10485760 | tf_op jit(solution)/shard_map/all_to_all | solution.py:565
  40.9 0.0 copy-done
  40.9 47.3 %evaluate.1 = s32[64,8,128]{2,1,0:T(8,128)S(1)} custom-call(s32[64,8,128]{2,1,0:T(8,128)S(1)} %bitcast.13, s32[1,128]{1,0:T(1,128)S(1)} %copy-done, bf16[1024,2560]{1,0:T(8,128)(2,1)} %file_hbm.1), custom_call_target="tpu_custom_call" | custom-call | flops 60000002048 | bytes 6000000 | tf_op jit(solution)/shard_map/evaluate/pallas_call | solution.py:441
  88.2 16.4 %all-to-all-done.1 = bf16[128,8,2560]{2,1,0:T(8,128)(2,1)} async-done(((bf16[128,8,2560]{2,1,0:T(8,128)(2,1)}), bf16[128,8,2560]{2,1,0:T(8,128)(2,1)}, u32[]{:S(2)}, u32[]{:S(2)}) %all-to-all-start.1) | async-done | bytes 5242912 | tf_op jit(solution)/shard_map/all_to_all | solution.py:565
  104.7 15.7 %all_to_all.15 = s32[128,4,128]{2,1,0:T(4,128)} all-to-all(s32[128,4,128]{2,1,0:T(4,128)S(1)} %bitcast.14), channel_id=1, replica_groups=mesh['owner'=64,'sub'=2] {'owner','sub'}, dimensions={0} | all-to-all | bytes 524288 | tf_op jit(solution)/shard_map/all_to_all | solution.py:565
  120.4 11.4 %collect.1 = (f32[5,16384]{1,0:T(8,128)}, bf16[1024,2560]{1,0:T(8,128)(2,1)}) custom-call(s32[64,8,128]{2,1,0:T(8,128)} %bitcast.16, s32[1,16384]{1,0:T(1,128)} %get-tuple-element.12.slot_ref, bf16[1024,2560]{1,0:T(8,128)(2,1)} %bitcast.7.moved_hbm), custom_call_target="tpu_custom_call" | custom-call | tf_op jit(solution)/shard_map/collect/pallas_call | solution.py:541
  (3 shorter events, 0.0 us)
Async XLA Ops:
  11.9 22.6 %all-to-all-start = ((s32[128,4,128]{2,1,0:T(4,128)}), s32[128,4,128]{2,1,0:T(4,128)S(1)}, u32[]{:S(2)}, u32[]{:S(2)}) async-start(s32[128,4,128]{2,1,0:T(4,128)} %bitcast.17), calls=%async_computation | async-start | bytes 524288 | tf_op jit(solution)/shard_map/all_to_all | solution.py:565
  34.4 6.5 %copy-start = (s32[1,128]{1,0:T(1,128)S(1)}, s32[1,128]{1,0:T(1,128)}, u32[]{:S(2)}) copy-start(s32[1,128]{1,0:T(1,128)} %span_ref.1) | copy-start | bytes 1540
  34.4 70.2 %all-to-all-start.1 = ((bf16[128,8,2560]{2,1,0:T(8,128)(2,1)}), bf16[128,8,2560]{2,1,0:T(8,128)(2,1)}, u32[]{:S(2)}, u32[]{:S(2)}) async-start(bf16[128,8,2560]{2,1,0:T(8,128)(2,1)} %gather_fusion), calls=%async_computation.1 | async-start | bytes 10485760 | tf_op jit(solution)/shard_map/all_to_all | solution.py:565

commit v6 on v5

--- a/solution.py
+++ b/solution.py
@@ -168,10 +168,14 @@
         slot = slot_ref[:, at(n)]
         where_row = onehot(0, ROWS, slot >> 8)
         where_col = onehot(0, 256, slot & 255)
-        rows = [both(where_row, *parts(to_grid(coords_ref[k : k + 1, at(n)]))) for k in range(3)]
-        rows.append(both(where_row, dest_ref[:, at(n)] * 8 + 8, local_ref[:, at(n)] & 7))
-        wide = jnp.concatenate([where_col, where_col], axis=1)
-        return lane_dot(jnp.concatenate(rows, axis=0), wide)
+        local = local_ref[:, at(n)]
+        rows = []
+        for k in range(3):
+            clear = (1 - ((local >> k) & 1)) * 65536
+            grid = to_grid(coords_ref[k : k + 1, at(n)]) - clear.astype(F32)
+            rows += [spread(where_row, part) for part in parts(grid)]
+        rows.append(spread(where_row, dest_ref[:, at(n)] + 1))
+        return lane_dot(jnp.concatenate(rows, axis=0), where_col)
 
     copies[0].wait()
     base = place(0, jnp.zeros((DEVICES, 1), F32))
@@ -186,11 +190,17 @@
 
     lax.fori_loop(0, steps - 1, step, base)
     acc_ref[...] += scatter(steps - 1)
+    fields = [acc_ref[k * ROWS : k * ROWS + ROWS, :].astype(I32) for k in range(7)]
+    fields = [fields[0] + fields[1], fields[2] + fields[3], fields[4] + fields[5], fields[6]]
+    number = fields[3] * 8
+    for k in range(3):
+        signed = fields[k] + 65536
+        number = number + ((signed >> 16) << k)
+        fields[k] = signed & 0xFFFF
+    fields[3] = jnp.where(fields[3] > 0, number, 0)
     middle = []
     for k in range(2):
-        low, high = [
-            acc_ref[q * ROWS : q * ROWS + ROWS, :].astype(I32) for q in (2 * k, 2 * k + 1)
-        ]
+        low, high = fields[2 * k], fields[2 * k + 1]
         block = low + (high << 16)
         flat_ref[pl.ds(0, ROWS, 2), :] = block[:, 0:128]
         flat_ref[pl.ds(1, ROWS, 2), :] = block[:, 128:256]
@@ -216,7 +226,7 @@
             pltpu.VMEM((1, POINTS), I32),
             pltpu.VMEM((1, POINTS), I32),
             pltpu.VMEM((3, POINTS), F32),
-            pltpu.VMEM((4 * ROWS, 256), F32),
+            pltpu.VMEM((7 * ROWS, 256), F32),
             pltpu.VMEM((2 * ROWS, 128), I32),
             pltpu.SemaphoreType.DMA((4,)),
         ],

time: 132 us -> 132 us (level)
  no operation moved by 1% of the time
where the time goes in v6:
time: 132 us; the launch traced here: 131 us
  Pallas kernels  69.3 us (52%)
  waiting for transfers between devices  20.1 us (15%)
  starting transfers between devices  18 us (14%)
  blocking collectives  15.7 us (12%)
  local copies, waits for them, and re-layouts  6.71 us (5%)
    pallas_call x1, Pallas kernels, evaluate(): pl.pallas_call(evaluate_kernel, out_shape=jax.ShapeDtypeStruct((DEVICES /...  47.3 us
    all_to_all x2, waiting for transfers between devices, exchange(): return lax.all_to_all(x, AXES, split_axis=0, concat_axis=0, tiled=True)  20.1 us
    all_to_all x2, starting transfers between devices, exchange(): return lax.all_to_all(x, AXES, split_axis=0, concat_axis=0, tiled=True)  18 us
    all_to_all x1, blocking collectives, exchange(): return lax.all_to_all(x, AXES, split_axis=0, concat_axis=0, tiled=True)  15.7 us
    pallas_call x1, Pallas kernels, collect(): pl.pallas_call(collect_kernel, out_shape=(jax.ShapeDtypeStruct((FIELDS, P...  11.4 us
    pallas_call x1, Pallas kernels, bucket(): pl.pallas_call(bucket_kernel, out_shape=(jax.ShapeDtypeStruct((DEVICES //...  10.6 us
    gather x1, local copies, waits for them, and re-layouts, shards(): pieces = file_fields.reshape(DEVICES, SPAN, WIDTH)[inverse]  5.73 us
  transfers between devices with their start and end apart: 2, of which 2 were waited for; matrix products, arithmetic and copies ran while one was open for 6% of the time, Pallas kernels for 36%

profile of v6, /device:TPU:1, one launch (start us, length us, event | category | flops | bytes accessed | tf_op | source)
XLA Modules:
  0.0 131.4 jit_solution(446746534526766093)
XLA Ops:
  0.6 10.6 %bucket.1 = (s32[64,8,128]{2,1,0:T(8,128)}, s32[1,16384]{1,0:T(1,128)}) custom-call(s32[1,16384]{1,0:T(1,128)} %bitcast.18, s32[1,16384]{1,0:T(1,128)} %bitcast.19, f32[3,16384]{1,0:T(4,128)} %coords_hbm.1), custom_call_target="tpu_custom_call" | custom-call | tf_op jit(solution)/shard_map/bucket/pallas_call | solution.py:217
  11.2 11.5 %all-to-all-start = ((s32[128,4,128]{2,1,0:T(4,128)}), s32[128,4,128]{2,1,0:T(4,128)S(1)}, u32[]{:S(2)}, u32[]{:S(2)}) async-start(s32[128,4,128]{2,1,0:T(4,128)} %bitcast.17), calls=%async_computation | async-start | bytes 524288 | tf_op jit(solution)/shard_map/all_to_all | solution.py:575
  22.7 0.7 fusion
  23.4 1.0 scatter_custom_fusion
  24.4 5.7 %gather_fusion = bf16[128,8,2560]{2,1,0:T(8,128)(2,1)} fusion(bf16[128,8,2560]{2,1,0:T(8,128)(2,1)} %bitcast.15, s32[1024]{0:T(1024)S(1)} %pad_clamp_fusion), kind=kCustom, calls=%fused_computation | custom fusion | bytes 10486272 | tf_op jit(solution)/shard_map/gather | solution.py:581
  30.1 3.7 %all-to-all-done = s32[128,4,128]{2,1,0:T(4,128)S(1)} async-done(((s32[128,4,128]{2,1,0:T(4,128)}), s32[128,4,128]{2,1,0:T(4,128)S(1)}, u32[]{:S(2)}, u32[]{:S(2)}) %all-to-all-start) | async-done | bytes 262176 | tf_op jit(solution)/shard_map/all_to_all | solution.py:575
  33.8 0.0 copy-start
  33.8 6.5 %all-to-all-start.1 = ((bf16[128,8,2560]{2,1,0:T(8,128)(2,1)}), bf16[128,8,2560]{2,1,0:T(8,128)(2,1)}, u32[]{:S(2)}, u32[]{:S(2)}) async-start(bf16[128,8,2560]{2,1,0:T(8,128)(2,1)} %gather_fusion), calls=%async_computation.1 | async-start | bytes 10485760 | tf_op jit(solution)/shard_map/all_to_all | solution.py:575
  40.3 0.0 copy-done
  40.3 47.3 %evaluate.1 = s32[64,8,128]{2,1,0:T(8,128)S(1)} custom-call(s32[64,8,128]{2,1,0:T(8,128)S(1)} %bitcast.13, s32[1,128]{1,0:T(1,128)S(1)} %copy-done, bf16[1024,2560]{1,0:T(8,128)(2,1)} %file_hbm.1), custom_call_target="tpu_custom_call" | custom-call | flops 60000002048 | bytes 6000000 | tf_op jit(solution)/shard_map/evaluate/pallas_call | solution.py:451
  87.6 16.5 %all-to-all-done.1 = bf16[128,8,2560]{2,1,0:T(8,128)(2,1)} async-done(((bf16[128,8,2560]{2,1,0:T(8,128)(2,1)}), bf16[128,8,2560]{2,1,0:T(8,128)(2,1)}, u32[]{:S(2)}, u32[]{:S(2)}) %all-to-all-start.1) | async-done | bytes 5242912 | tf_op jit(solution)/shard_map/all_to_all | solution.py:575
  104.0 15.7 %all_to_all.15 = s32[128,4,128]{2,1,0:T(4,128)} all-to-all(s32[128,4,128]{2,1,0:T(4,128)S(1)} %bitcast.14), channel_id=1, replica_groups=mesh['owner'=64,'sub'=2] {'owner','sub'}, dimensions={0} | all-to-all | bytes 524288 | tf_op jit(solution)/shard_map/all_to_all | solution.py:575
  119.8 11.4 %collect.1 = (f32[5,16384]{1,0:T(8,128)}, bf16[1024,2560]{1,0:T(8,128)(2,1)}) custom-call(s32[64,8,128]{2,1,0:T(8,128)} %bitcast.16, s32[1,16384]{1,0:T(1,128)} %get-tuple-element.12.slot_ref, bf16[1024,2560]{1,0:T(8,128)(2,1)} %bitcast.7.moved_hbm), custom_call_target="tpu_custom_call" | custom-call | tf_op jit(solution)/shard_map/collect/pallas_call | solution.py:551
  (3 shorter events, 0.0 us)
Async XLA Ops:
  11.2 22.6 %all-to-all-start = ((s32[128,4,128]{2,1,0:T(4,128)}), s32[128,4,128]{2,1,0:T(4,128)S(1)}, u32[]{:S(2)}, u32[]{:S(2)}) async-start(s32[128,4,128]{2,1,0:T(4,128)} %bitcast.17), calls=%async_computation | async-start | bytes 524288 | tf_op jit(solution)/shard_map/all_to_all | solution.py:575
  33.8 6.5 %copy-start = (s32[1,128]{1,0:T(1,128)S(1)}, s32[1,128]{1,0:T(1,128)}, u32[]{:S(2)}) copy-start(s32[1,128]{1,0:T(1,128)} %span_ref.1) | copy-start | bytes 1540
  33.8 70.2 %all-to-all-start.1 = ((bf16[128,8,2560]{2,1,0:T(8,128)(2,1)}), bf16[128,8,2560]{2,1,0:T(8,128)(2,1)}, u32[]{:S(2)}, u32[]{:S(2)}) async-start(bf16[128,8,2560]{2,1,0:T(8,128)(2,1)} %gather_fusion), calls=%async_computation.1 | async-start | bytes 10485760 | tf_op jit(solution)/shard_map/all_to_all | solution.py:575

commit v7 on v6

--- a/solution.py
+++ b/solution.py
@@ -99,6 +99,23 @@
         base = base + inside[:, 255:256] + ones[:, 256 * j + 255 : 256 * j + 256]
     count = jnp.concatenate(counts, axis=1)
     return jnp.sum(jnp.where(mask, count, 0.0), axis=0, keepdims=True), base
+
+
+def small_ranks(ones, before, base):
+    rows, blocks = ones.shape[0], ones.shape[1] // 256
+    parts_of = [ones[:, 256 * j : 256 * j + 256] for j in range(blocks)]
+    stacked = dot(jnp.concatenate(parts_of, axis=0), before)
+    out = []
+    for j in range(blocks):
+        inside = stacked[rows * j : rows * j + rows]
+        count = inside.astype(BF16) + jnp.broadcast_to(base, (rows, 256)).astype(BF16)
+        picked = parts_of[j] * count
+        total = picked[0:16]
+        for r in range(1, rows // 16):
+            total = total + picked[16 * r : 16 * r + 16]
+        out.append(jnp.sum(total.astype(F32), axis=0, keepdims=True))
+        base = base + inside[:, 255:256] + parts_of[j][:, 255:256].astype(F32)
+    return jnp.concatenate(out, axis=1), base
 
 
 def flat_slot(block, place):
@@ -160,7 +177,7 @@
 
     def place(n, base):
         holder = local_ref[:, at(n)] >> 3
-        rank, base = ranks(iota((DEVICES, A_LANES), 0) == holder, before, base)
+        rank, base = small_ranks(onehot(0, DEVICES, holder), before, base)
         slot_ref[:, at(n)] = flat_slot(holder, rank.astype(I32))
         return base
 

time: 132 us -> 131 us (level)
  no operation moved by 1% of the time
where the time goes in v7:
time: 131 us
  Pallas kernels  68.7 us (52%)
  waiting for transfers between devices  20.1 us (15%)
  starting transfers between devices  18 us (14%)
  blocking collectives  15.7 us (12%)
  local copies, waits for them, and re-layouts  6.71 us (5%)
    pallas_call x1, Pallas kernels, evaluate(): pl.pallas_call(evaluate_kernel, out_shape=jax.ShapeDtypeStruct((DEVICES /...  47.3 us
    all_to_all x2, waiting for transfers between devices, exchange(): return lax.all_to_all(x, AXES, split_axis=0, concat_axis=0, tiled=True)  20.1 us
    all_to_all x2, starting transfers between devices, exchange(): return lax.all_to_all(x, AXES, split_axis=0, concat_axis=0, tiled=True)  18 us
    all_to_all x1, blocking collectives, exchange(): return lax.all_to_all(x, AXES, split_axis=0, concat_axis=0, tiled=True)  15.7 us
    pallas_call x1, Pallas kernels, collect(): pl.pallas_call(collect_kernel, out_shape=(jax.ShapeDtypeStruct((FIELDS, P...  11.4 us
    pallas_call x1, Pallas kernels, bucket(): pl.pallas_call(bucket_kernel, out_shape=(jax.ShapeDtypeStruct((DEVICES //...  9.95 us
    gather x1, local copies, waits for them, and re-layouts, shards(): pieces = file_fields.reshape(DEVICES, SPAN, WIDTH)[inverse]  5.73 us
  transfers between devices with their start and end apart: 2, of which 2 were waited for; matrix products, arithmetic and copies ran while one was open for 6% of the time, Pallas kernels for 36%

profile of v7, /device:TPU:1, one launch (start us, length us, event | category | flops | bytes accessed | tf_op | source)
XLA Modules:
  0.0 130.7 jit_solution(15243934853546630488)
XLA Ops:
  0.6 9.9 %bucket.1 = (s32[64,8,128]{2,1,0:T(8,128)}, s32[1,16384]{1,0:T(1,128)}) custom-call(s32[1,16384]{1,0:T(1,128)} %bitcast.18, s32[1,16384]{1,0:T(1,128)} %bitcast.19, f32[3,16384]{1,0:T(4,128)} %coords_hbm.1), custom_call_target="tpu_custom_call" | custom-call | tf_op jit(solution)/shard_map/bucket/pallas_call | solution.py:234
  10.6 11.5 %all-to-all-start = ((s32[128,4,128]{2,1,0:T(4,128)}), s32[128,4,128]{2,1,0:T(4,128)S(1)}, u32[]{:S(2)}, u32[]{:S(2)}) async-start(s32[128,4,128]{2,1,0:T(4,128)} %bitcast.17), calls=%async_computation | async-start | bytes 524288 | tf_op jit(solution)/shard_map/all_to_all | solution.py:592
  22.1 0.7 fusion
  22.7 1.0 scatter_custom_fusion
  23.7 5.7 %gather_fusion = bf16[128,8,2560]{2,1,0:T(8,128)(2,1)} fusion(bf16[128,8,2560]{2,1,0:T(8,128)(2,1)} %bitcast.15, s32[1024]{0:T(1024)S(1)} %pad_clamp_fusion), kind=kCustom, calls=%fused_computation | custom fusion | bytes 10486272 | tf_op jit(solution)/shard_map/gather | solution.py:598
  29.5 3.7 %all-to-all-done = s32[128,4,128]{2,1,0:T(4,128)S(1)} async-done(((s32[128,4,128]{2,1,0:T(4,128)}), s32[128,4,128]{2,1,0:T(4,128)S(1)}, u32[]{:S(2)}, u32[]{:S(2)}) %all-to-all-start) | async-done | bytes 262176 | tf_op jit(solution)/shard_map/all_to_all | solution.py:592
  33.2 0.0 copy-start
  33.2 6.5 %all-to-all-start.1 = ((bf16[128,8,2560]{2,1,0:T(8,128)(2,1)}), bf16[128,8,2560]{2,1,0:T(8,128)(2,1)}, u32[]{:S(2)}, u32[]{:S(2)}) async-start(bf16[128,8,2560]{2,1,0:T(8,128)(2,1)} %gather_fusion), calls=%async_computation.1 | async-start | bytes 10485760 | tf_op jit(solution)/shard_map/all_to_all | solution.py:592
  39.7 0.0 copy-done
  39.7 47.3 %evaluate.1 = s32[64,8,128]{2,1,0:T(8,128)S(1)} custom-call(s32[64,8,128]{2,1,0:T(8,128)S(1)} %bitcast.13, s32[1,128]{1,0:T(1,128)S(1)} %copy-done, bf16[1024,2560]{1,0:T(8,128)(2,1)} %file_hbm.1), custom_call_target="tpu_custom_call" | custom-call | flops 60000002048 | bytes 6000000 | tf_op jit(solution)/shard_map/evaluate/pallas_call | solution.py:468
  87.0 16.5 %all-to-all-done.1 = bf16[128,8,2560]{2,1,0:T(8,128)(2,1)} async-done(((bf16[128,8,2560]{2,1,0:T(8,128)(2,1)}), bf16[128,8,2560]{2,1,0:T(8,128)(2,1)}, u32[]{:S(2)}, u32[]{:S(2)}) %all-to-all-start.1) | async-done | bytes 5242912 | tf_op jit(solution)/shard_map/all_to_all | solution.py:592
  103.4 15.7 %all_to_all.15 = s32[128,4,128]{2,1,0:T(4,128)} all-to-all(s32[128,4,128]{2,1,0:T(4,128)S(1)} %bitcast.14), channel_id=1, replica_groups=mesh['owner'=64,'sub'=2] {'owner','sub'}, dimensions={0} | all-to-all | bytes 524288 | tf_op jit(solution)/shard_map/all_to_all | solution.py:592
  119.1 11.4 %collect.1 = (f32[5,16384]{1,0:T(8,128)}, bf16[1024,2560]{1,0:T(8,128)(2,1)}) custom-call(s32[64,8,128]{2,1,0:T(8,128)} %bitcast.16, s32[1,16384]{1,0:T(1,128)} %get-tuple-element.12.slot_ref, bf16[1024,2560]{1,0:T(8,128)(2,1)} %bitcast.7.moved_hbm), custom_call_target="tpu_custom_call" | custom-call | tf_op jit(solution)/shard_map/collect/pallas_call | solution.py:568
  (3 shorter events, 0.0 us)
Async XLA Ops:
  10.6 22.6 %all-to-all-start = ((s32[128,4,128]{2,1,0:T(4,128)}), s32[128,4,128]{2,1,0:T(4,128)S(1)}, u32[]{:S(2)}, u32[]{:S(2)}) async-start(s32[128,4,128]{2,1,0:T(4,128)} %bitcast.17), calls=%async_computation | async-start | bytes 524288 | tf_op jit(solution)/shard_map/all_to_all | solution.py:592
  33.2 6.5 %copy-start = (s32[1,128]{1,0:T(1,128)S(1)}, s32[1,128]{1,0:T(1,128)}, u32[]{:S(2)}) copy-start(s32[1,128]{1,0:T(1,128)} %span_ref.1) | copy-start | bytes 1540
  33.2 70.2 %all-to-all-start.1 = ((bf16[128,8,2560]{2,1,0:T(8,128)(2,1)}), bf16[128,8,2560]{2,1,0:T(8,128)(2,1)}, u32[]{:S(2)}, u32[]{:S(2)}) async-start(bf16[128,8,2560]{2,1,0:T(8,128)(2,1)} %gather_fusion), calls=%async_computation.1 | async-start | bytes 10485760 | tf_op jit(solution)/shard_map/all_to_all | solution.py:592
